TPU v7x, 512 devices: a whole 4x4x16 slice. The times are simulated.
512 devices in a mesh: row: 16 (over x, y), col: 32 (over z, core).
Axes of the slice: x: 4, y: 4, z: 16, core: 2. Of those that a mesh axis runs over, the one named last changes fastest.
Arguments:
- blocks: float32 [16, 32, 64, 128, 128], P('row', 'col')
- block_rows: int32 [16, 32, 64], P('row', 'col'), may hold values from 0 to 31
- block_cols: int32 [16, 32, 64], P('row', 'col'), may hold values from 0 to 15
- block_valid: int32 [16, 32, 64], P('row', 'col'), may hold values from 0 to 1, as said below
- rhs: float32 [16, 32, 64, 128], P('row', 'col')
Outputs:
- solution: float32 [16, 32, 64, 128], P('row', 'col')
Inputs may be any that keep to these rules, and one draw needn't show every extreme that they name: `block_valid`: in each device's list the valid slots come first; every device has at least 16 valid slots, and at least one device has all 64 slots valid.
All inputs are finite; a program needn't handle non-finite values.
Results may differ from a plain program's by a relative error of at most 0.0003.
Values sent between devices are 32-bit elements; how exact they have to be, the bound alone decides.
No kernel may reach another device: no remote copies, remote signals or barrier semaphores. Data moves between devices by JAX's collectives and lax.ppermute only.
A program may use at most 64 MiB of HBM per device.

v0:
```python
import jax
import jax.numpy as jnp
from jax import lax
from jax.sharding import PartitionSpec as P

RBL = 32
CBL = 16
ITERS = 2


HIGH = lax.Precision.HIGHEST
eps = 1e-06


def root(total):
    return jnp.sqrt(total + eps)


def advance(state, vec, alpha, beta):
    x_vec, w_vec, phibar, rhobar = state
    rho = jnp.sqrt(rhobar * rhobar + beta * beta)
    cosine = rhobar / rho
    sine = beta / rho
    theta = sine * alpha
    rhobar = -cosine * alpha
    phi = cosine * phibar
    phibar = sine * phibar
    x_vec = x_vec + (phi / rho)[:, None] * w_vec
    w_vec = vec - (theta / rho)[:, None] * w_vec
    return (x_vec, w_vec, phibar, rhobar)


def on_device(blocks, block_rows, block_cols, block_valid, rhs):
    mats = blocks[0, 0]
    rows = block_rows[0, 0]
    cols = block_cols[0, 0]
    valid = block_valid[0, 0].astype(jnp.float32)
    width = mats.shape[1]
    piece = rhs[0, 0]
    count = piece.shape[0]
    row_map = (rows[:, None] == jnp.arange(RBL, dtype=jnp.int32)[None, :]).astype(
        jnp.float32
    ) * valid[:, None]
    col_map = (cols[:, None] == jnp.arange(CBL, dtype=jnp.int32)[None, :]).astype(
        jnp.float32
    ) * valid[:, None]

    def backward(ufull):
        tiles = jnp.take(ufull.reshape(count, RBL, width), rows, axis=1)
        prod = jnp.einsum("sab,ksa->ksb", mats, tiles, precision=HIGH)
        return jnp.einsum("sc,ksb->kcb", col_map, prod, precision=HIGH).reshape(count, CBL * width)

    beta = root(lax.psum(jnp.sum(piece * piece, axis=1), ("row", "col")))

    def to_cols(ufull, vfull, scale):
        fresh = lax.psum(backward(ufull), "row") - scale[:, None] * vfull
        alpha = root(lax.psum(jnp.sum(fresh * fresh, axis=1), "col"))
        return (fresh / alpha[:, None], alpha)

    urow = lax.all_gather(piece, "col", axis=1, tiled=True)
    u_vec = urow / beta[:, None]
    v_vec, alpha = to_cols(u_vec, jnp.zeros((count, CBL * width), jnp.float32), beta)
    state = (jnp.zeros_like(v_vec), v_vec, beta, alpha)
    for step_index in range(ITERS):
        forward_tiles = jnp.take(v_vec.reshape(count, CBL, width), cols, axis=1)
        forward_prod = jnp.einsum("sab,ksb->ksa", mats, forward_tiles, precision=HIGH)
        to_fresh = (
            lax.psum(
                jnp.einsum("sr,ksa->kra", row_map, forward_prod, precision=HIGH).reshape(
                    count, RBL * width
                ),
                "col",
            )
            - alpha[:, None] * u_vec
        )
        to_scale = root(lax.psum(jnp.sum(to_fresh * to_fresh, axis=1), "row"))
        u_vec = to_fresh / to_scale[:, None]
        beta = to_scale
        v_vec, alpha = to_cols(u_vec, v_vec, beta)
        state = advance(state, v_vec, alpha, beta)
    share = CBL * width // lax.axis_size("row")
    x_out = lax.dynamic_slice_in_dim(state[0], lax.axis_index("row") * share, share, 1)
    return x_out[None, None]


def solution(mesh):
    placed = (
        P("row", "col", None, None, None),
        P("row", "col", None),
        P("row", "col", None),
        P("row", "col", None),
        P("row", "col", None, None),
    )
    return jax.shard_map(
        on_device,
        mesh=mesh,
        in_specs=placed,
        out_specs=P("row", "col", None, None),
        check_vma=False,
    )
```

profile of v0, /device:TPU:1, one launch (start us, length us, event | category | flops | bytes accessed | tf_op | source)
XLA Modules:
  0.0 996.1 jit_solution(8083474009869830411)
XLA Ops:
  8.2 111.2 %psum.63 = f32[64]{0:T(128)S(1)} all-reduce(f32[64]{0:T(128)S(1)} %multiply_reduce_fusion.4), channel_id=1, replica_groups=mesh['row'=16,'col'=32] {'row','col'}, use_global_device_ids=true, to_apply=%region_1.0 | all-reduce | flops 64 | bytes 512 | tf_op jit(solution)/shard_map/psum | solution.py:53
  121.4 1.4 copy_bitcast_fusion.3
  123.5 5.7 fusion.24
  129.2 2.4 fusion.18
  132.6 107.6 %all-reduce.5.cloned.1.call-done = f32[64,2048]{1,0:T(8,128)} async-done(((f32[64,2048]{1,0:T(8,128)}), f32[64,2048]{1,0:T(8,128)}) %all-reduce.5.cloned.1.call-update) | async-done | bytes 524304 | tf_op jit(solution)/shard_map/psum | solution.py:56
  241.5 48.5 %psum.65 = f32[64]{0:T(128)S(1)} all-reduce(f32[64]{0:T(128)S(1)} %multiply_reduce_fusion.3), channel_id=1, replica_groups=mesh['row'=16,'col'=32] {'col'}, use_global_device_ids=true, to_apply=%region_4.6 | all-reduce | flops 64 | bytes 512 | tf_op jit(solution)/shard_map/psum | solution.py:57
  291.9 9.8 fusion.29
  301.7 2.5 fusion.16
  304.2 1.6 copy.39
  305.9 208.9 %all-reduce.7.cloned.1.call-done = f32[64,4096]{1,0:T(8,128)} async-done(((f32[64,4096]{1,0:T(8,128)}), f32[64,4096]{1,0:T(8,128)}) %all-reduce.7.cloned.1.call-update) | async-done | bytes 1048592 | tf_op jit(solution)/shard_map/psum | solution.py:68
  514.7 1.6 multiply_reduce_fusion.1
  516.3 33.3 %psum.67 = f32[64]{0:T(128)S(1)} all-reduce(f32[64]{0:T(128)S(1)} %get-tuple-element.12), channel_id=1, replica_groups=mesh['row'=16,'col'=32] {'row'}, use_global_device_ids=true, to_apply=%region_7.10 | all-reduce | flops 64 | bytes 512 | tf_op jit(solution)/shard_map/psum | solution.py:76
  549.8 2.0 gather_fusion.2
  551.9 6.0 fusion.34
  557.9 2.4 fusion.14
  561.5 116.3 %all-reduce.9.cloned.1.call-done = f32[64,2048]{1,0:T(8,128)} async-done(((f32[64,2048]{1,0:T(8,128)}), f32[64,2048]{1,0:T(8,128)}) %all-reduce.9.cloned.1.call-update) | async-done | bytes 524304 | tf_op jit(solution)/shard_map/psum | solution.py:56
  679.2 48.3 %psum.69 = f32[64]{0:T(128)S(1)} all-reduce(f32[64]{0:T(128)S(1)} %multiply_reduce_fusion.2), channel_id=1, replica_groups=mesh['row'=16,'col'=32] {'col'}, use_global_device_ids=true, to_apply=%region_10.13 | all-reduce | flops 64 | bytes 512 | tf_op jit(solution)/shard_map/psum | solution.py:57
  728.8 2.0 gather_fusion.3
  730.9 10.1 %fusion.39 = f32[64,64,128]{2,0,1:T(8,128)S(1)} fusion(f32[1,1,64,128,128]{4,3,2,1,0:T(8,128)} %param.9, f32[64,64,128]{2,1,0:T(8,128)} %gather_fusion.3, pred[64]{0:T(512)(128)(4,1)S(1)} %get-tuple-element.17), kind=kOutput, calls=%fused_computation.31 | convolution fusion | flops 805830656 | bytes 8388672 | tf_op jit(solution)/shard_map/sab,ksb->ksa/dot_general | solution.py:66
  740.9 2.5 fusion.12
  743.4 1.6 copy.38
  745.2 208.8 %all-reduce.11.cloned.1.call-done = f32[64,4096]{1,0:T(8,128)} async-done(((f32[64,4096]{1,0:T(8,128)}), f32[64,4096]{1,0:T(8,128)}) %all-reduce.11.cloned.1.call-update) | async-done | bytes 1048592 | tf_op jit(solution)/shard_map/psum | solution.py:68
  954.0 1.6 multiply_reduce_fusion
  955.5 33.3 %psum.71 = f32[64]{0:T(128)S(1)} all-reduce(f32[64]{0:T(128)S(1)} %multiply_reduce_fusion), channel_id=1, replica_groups=mesh['row'=16,'col'=32] {'row'}, use_global_device_ids=true, to_apply=%region_13.16 | all-reduce | flops 64 | bytes 512 | tf_op jit(solution)/shard_map/psum | solution.py:76
  (44 shorter events, 13.5 us)
Async XLA Ops:
  6.5 114.8 %all-gather.3.cloned.1.call-start = ((), (), s32[]{:S(2)}) async-start(), calls=%async_computation.4 | async-start | bytes 1081344 | tf_op jit(solution)/shard_map/all_gather | solution.py:60
  7.3 233.0 %all-reduce.5.cloned.1.call-start = ((), (), s32[]{:S(2)}) async-start(), calls=%async_computation | async-start | bytes 1048576 | tf_op jit(solution)/shard_map/psum | solution.py:56
  123.5 5.7 copy-start.2
  132.5 382.2 %all-reduce.7.cloned.1.call-start = ((), (), s32[]{:S(2)}) async-start(), calls=%async_computation.1 | async-start | bytes 2097152 | tf_op jit(solution)/shard_map/psum | solution.py:68
  291.9 9.8 copy-start.3
  304.2 210.5 %copy-start.1 = (f32[1,1,64,4096]{3,2,1,0:T(8,128)S(1)}, f32[1,1,64,4096]{3,2,1,0:T(8,128)}, u32[]{:S(2)}) copy-start(f32[1,1,64,4096]{3,2,1,0:T(8,128)} %all-gather.3.cloned.1.call-done) | copy-start | bytes 3145732
  305.8 372.0 %all-reduce.9.cloned.1.call-start = ((), (), s32[]{:S(2)}) async-start(), calls=%async_computation.2 | async-start | bytes 1048576 | tf_op jit(solution)/shard_map/psum | solution.py:56
  557.9 119.9 %copy-start = (f32[64,2048]{1,0:T(8,128)S(1)}, f32[64,2048]{1,0:T(8,128)}, u32[]{:S(2)}) copy-start(f32[64,2048]{1,0:T(8,128)} %all-reduce.5.cloned.1.call-done) | copy-start | bytes 1572868
  561.3 392.7 %all-reduce.11.cloned.1.call-start = ((), (), s32[]{:S(2)}) async-start(), calls=%async_computation.3 | async-start | bytes 2097152 | tf_op jit(solution)/shard_map/psum | solution.py:68
Sparse Core Ops, SparseCore 0:
  9.4 75.9 all-gather.2
  132.7 107.5 all-reduce.4
  305.9 208.7 all-reduce.6
  561.4 116.3 all-reduce.8
  745.2 208.7 all-reduce.10
where the time goes:
time: 1000 us; the launch traced here: 996 us
  waiting for transfers between devices  642 us (64%)
  blocking collectives  275 us (28%)
  matrix products  41.2 us (4%)
  other arithmetic  13.5 us (1%)
  between operations  13.4 us (1%)
  local copies, waits for them, and re-layouts  10.7 us (1%)
    psum x2, waiting for transfers between devices, on_device(): lax.psum(jnp.einsum('sr,ksa->kra', row_map, forward_prod, precision=HIGH)...  418 us
    psum x2, waiting for transfers between devices, to_cols(): fresh = lax.psum(backward(ufull), 'row') - scale[:, None] * vfull  224 us
    psum x1, blocking collectives, on_device(): beta = root(lax.psum(jnp.sum(piece * piece, axis=1), ('row', 'col')))  111 us
    psum x2, blocking collectives, to_cols(): alpha = root(lax.psum(jnp.sum(fresh * fresh, axis=1), 'col'))  96.8 us
    psum x2, blocking collectives, on_device(): to_scale = root(lax.psum(jnp.sum(to_fresh * to_fresh, axis=1), 'row'))  66.7 us
  transfers between devices with their start and end apart: 5, of which 4 were waited for; matrix products, arithmetic and copies ran while one was open for 0% of the time, Pallas kernels for 0%

commit v1 on v0

v1 whole, which is shorter than its diff:
```python
import jax
import jax.numpy as jnp
from jax import lax
from jax.experimental import pallas as pl
from jax.experimental.pallas import tpu as pltpu
from jax.sharding import Mesh, PartitionSpec as P

W = 128
SLOTS = 64
RBL = 32
CBL = 16
NZ = 16
ITERS = 2
PAD = 8
eps = 1e-06
SCALE = 0.25

F32 = jnp.float32
BF16 = jnp.bfloat16
NT = (((1,), (1,)), ((), ()))

SMEM = pl.BlockSpec(memory_space=pltpu.SMEM)
VMEM = pl.BlockSpec(memory_space=pltpu.VMEM)
PARAMS = pltpu.CompilerParams(vmem_limit_bytes=32 << 20)


def root(total):
    return jnp.sqrt(total + eps)


def halves(x):
    hi = x.astype(BF16)
    return hi, (x - hi.astype(F32)).astype(BF16)


def diagonal(count):
    shape = (count, W)
    return lax.broadcasted_iota(jnp.int32, shape, 0) == lax.broadcasted_iota(jnp.int32, shape, 1)


def to_row(col):
    return jnp.sum(jnp.where(diagonal(col.shape[0]), col, 0.0), axis=0, keepdims=True)


def to_col(row, count):
    return jnp.sum(jnp.where(diagonal(count), row, 0.0), axis=1, keepdims=True)


def spread(col):
    return jnp.broadcast_to(col, (col.shape[0], W))


def norm_rows(squares):
    return jnp.broadcast_to(to_row(jnp.sum(squares, axis=1, keepdims=True)), (PAD, W))


def backward_kernel(rows, cols, valid, core, mats, own, other, out, parts, acc):
    me = core[0]
    count = own.shape[1]
    squares = jnp.zeros((count, W), F32)
    for z in range(NZ):
        for ref, c in ((own, me), (other, 1 - me)):
            x = ref[z]
            squares += x * x
            parts[2 * z + c] = jnp.concatenate(halves(x * SCALE), axis=1)
    acc[...] = jnp.zeros_like(acc)
    for s in range(SLOTS):
        target = jnp.where(valid[s] > 0, cols[s], CBL)
        hi, lo = halves(mats[s])
        u = parts[rows[s]]
        prod = jnp.dot(u, jnp.concatenate([hi, hi], axis=0), preferred_element_type=F32)
        prod += jnp.dot(u[:, :W], lo, preferred_element_type=F32)
        acc[target] += prod
    out[:, :count, :] = acc[:CBL]
    out[:, count:, :] = jnp.broadcast_to(norm_rows(squares)[None], (CBL, PAD, W))


def forward_kernel(rows, cols, valid, core, mats, vec, mine, theirs, parts, acc):
    me = core[0]
    count = vec.shape[1]
    squares = jnp.zeros((count, W), F32)
    for c in range(CBL):
        x = vec[c]
        squares += x * x
        parts[c] = jnp.concatenate(halves(x * SCALE), axis=1)
    acc[...] = jnp.zeros_like(acc)
    for s in range(SLOTS):
        target = jnp.where(valid[s] > 0, rows[s], RBL)
        hi, lo = halves(mats[s])
        v = parts[cols[s]]
        prod = lax.dot_general(v, jnp.concatenate([hi, hi], axis=1), NT, preferred_element_type=F32)
        prod += lax.dot_general(v[:, :W], lo, NT, preferred_element_type=F32)
        acc[target] += prod
    norms = norm_rows(squares)
    for z in range(NZ):
        mine[z, :count] = acc[2 * z + me]
        theirs[z, :count] = acc[2 * z + 1 - me]
        mine[z, count:] = norms
        theirs[z, count:] = norms


def gathered(got, count):
    total = got[0]
    for index in range(1, got.shape[0]):
        total += got[index]
    return total[:count], root(to_col(total[count : count + 1], count))


def first_cols_kernel(got, copies, fresh, scale):
    count = fresh.shape[0]
    total, beta = gathered(got, count)
    vec = total / (SCALE * beta)
    fresh[...] = vec
    copies[...] = jnp.broadcast_to(vec[None], copies.shape)
    scale[...] = spread(beta)


def cols_kernel(got, old, alpha, copies, fresh, scale):
    count = fresh.shape[0]
    total, beta = gathered(got, count)
    vec = total / (SCALE * beta) - beta * (old[...] / alpha[...])
    fresh[...] = vec
    copies[...] = jnp.broadcast_to(vec[None], copies.shape)
    scale[...] = spread(beta)


def rows_kernel(got, old, beta, fresh, scale, norms):
    count = fresh.shape[0]
    total, alpha = gathered(got, count)
    vec = total / (SCALE * alpha) - alpha * (old[...] / beta[...])
    fresh[...] = vec
    scale[...] = spread(alpha)
    norms[...] = norm_rows(vec * vec)


def total_kernel(got, scale):
    count = scale.shape[0]
    total = got[0]
    for index in range(1, got.shape[0]):
        total += got[index]
    scale[...] = spread(root(to_col(total[:1], count)))


def call(kernel, name, specs, outs, scratch=()):
    return pl.pallas_call(
        kernel,
        out_shape=outs,
        in_specs=specs,
        out_specs=jax.tree.map(lambda _: VMEM, outs),
        scratch_shapes=scratch,
        compiler_params=PARAMS,
        name=name,
    )


def array(*shape):
    return jax.ShapeDtypeStruct(shape, F32)


def advance(state, vec, alpha, beta):
    x_vec, w_vec, phibar, rhobar = state
    rho = jnp.sqrt(rhobar * rhobar + beta * beta)
    cosine = rhobar / rho
    sine = beta / rho
    theta = sine * alpha
    rhobar = -cosine * alpha
    phi = cosine * phibar
    phibar = sine * phibar
    x_vec = x_vec + (phi / rho) * w_vec
    w_vec = vec - (theta / rho) * w_vec
    return (x_vec, w_vec, phibar, rhobar)


def on_device(blocks, block_rows, block_cols, block_valid, rhs):
    mats = blocks[0, 0]
    piece = rhs[0, 0]
    count = piece.shape[0]
    core = lax.axis_index("core").astype(jnp.int32).reshape(1)
    slots = (block_rows[0, 0], block_cols[0, 0], block_valid[0, 0], core, mats)
    swap = [(0, 1), (1, 0)]
    tile, wide = array(count, W), array(NZ, count + PAD, W)
    copied = array(CBL, count, W)

    def exchange(x, axis):
        return lax.all_to_all(x, axis, 0, 0, tiled=True)

    def backward(u_piece):
        own = lax.all_gather(u_piece, "z")
        other = lax.ppermute(own, "core", swap)
        scratch = (pltpu.VMEM((RBL, count, 2 * W), BF16), pltpu.VMEM((CBL + 1, count, W), F32))
        specs = [SMEM] * 4 + [VMEM] * 3
        part = call(backward_kernel, "apply_transposed", specs, wide, scratch)(*slots, own, other)
        return exchange(part, "row")

    def forward(copies):
        vec = exchange(copies, "row")
        scratch = (pltpu.VMEM((CBL, count, 2 * W), BF16), pltpu.VMEM((RBL + 1, count, W), F32))
        specs = [SMEM] * 4 + [VMEM] * 2
        mine, theirs = call(forward_kernel, "apply_plain", specs, (wide, wide), scratch)(*slots, vec)
        return exchange(mine + lax.ppermute(theirs, "core", swap), "z")

    def everywhere(norms):
        norms = lax.psum(norms, "core")
        for axis, length in (("z", NZ), ("row", 16)):
            norms = exchange(jnp.broadcast_to(norms[None], (length, PAD, W)), axis)
            if axis == "z":
                norms = jnp.sum(norms, axis=0)
        return call(total_kernel, "total", [VMEM], tile)(norms)

    u_old = piece
    got = backward(u_old)
    copies, v_old, beta = call(first_cols_kernel, "first_cols", [VMEM], (copied, tile, tile))(got)
    state = None
    for step_index in range(ITERS):
        got = forward(copies)
        outs = (tile, tile, array(PAD, W))
        u_old, alpha, norms = call(rows_kernel, "rows", [VMEM] * 3, outs)(got, u_old, beta)
        v_now = v_old / alpha
        if state is None:
            state = (jnp.zeros_like(v_now), v_now, beta, alpha)
        else:
            state = advance(state, v_now, alpha, beta)
        got = backward(u_old)
        copies, v_old, beta = call(cols_kernel, "cols", [VMEM] * 3, (copied, tile, tile))(got, v_old, alpha)
    beta = everywhere(norms)
    squares = jnp.sum(v_old * v_old, axis=1)
    alpha = everywhere(jnp.broadcast_to(jnp.pad(squares, (0, W - count)), (PAD, W)))
    x_out = advance(state, v_old / alpha, alpha, beta)[0]
    return x_out[None, None]


def solution(mesh):
    grid = Mesh(mesh.devices.reshape(16, NZ, 2), ("row", "z", "core"))
    col = ("z", "core")
    placed = (
        P("row", col, None, None, None),
        P("row", col, None),
        P("row", col, None),
        P("row", col, None),
        P("row", col, None, None),
    )
    return jax.shard_map(
        on_device,
        mesh=grid,
        in_specs=placed,
        out_specs=P("row", col, None, None),
        check_vma=False,
    )
```

time: 1000 us -> 277 us (0.28)
  waiting for transfers between devices: 642 us -> 6.24 us
  blocking collectives: 275 us -> 220 us
  matrix products: 41.2 us -> 0 us
  starting transfers between devices: 0.39 us -> 30.8 us
  Pallas kernels: 0 us -> 13.3 us
  between operations: 13.4 us -> 0.14 us
  other arithmetic: 13.5 us -> 0.83 us
    psum x4 -> x0, waiting for transfers between devices: 642 us -> none  [the longest x2 418 us: on_device(): lax.psum(jnp.einsum('sr,ksa->kra', row_map, forward_prod, precision=HIGH)...]
    psum x5 -> x1, blocking collectives: 275 us -> 4.31 us  [everywhere(): norms = lax.psum(norms, 'core')]
    all_to_all x0 -> x8, blocking collectives: none -> 159 us  [exchange(): return lax.all_to_all(x, axis, 0, 0, tiled=True)]
    all_gather x0 -> x2, blocking collectives: none -> 56.2 us  [backward(): own = lax.all_gather(u_piece, 'z')]
    dot_general x8 -> x0, matrix products: 41.2 us -> none  [the longest x2 19.8 us: on_device(): jnp.einsum('sab,ksb->ksa', mats, forward_tiles, precision=HIGH)]
    ppermute x0 -> x4, starting transfers between devices: none -> 30.8 us  [the longest x2 20.5 us: backward(): other = lax.ppermute(own, 'core', swap)]
    pallas_call x0 -> x9, Pallas kernels: none -> 13.3 us  [the longest x2 7.39 us: forward(): call(forward_kernel, 'apply_plain', specs, (wide, wide), scratch)]
  transfers between devices with their start and end apart: 5 -> 4, of which waited for: 4 -> 4; matrix products, arithmetic and copies ran while one was open for 0% -> 0% of each run, Pallas kernels for 0% -> 0%
where the time goes in v1:
time: 277 us; the launch traced here: 275 us
  blocking collectives  220 us (79%)
  starting transfers between devices  30.8 us (11%)
  Pallas kernels  13.3 us (5%)
  waiting for transfers between devices  6.24 us (2%)
  local copies, waits for them, and re-layouts  4.19 us (2%)
    all_to_all x8, blocking collectives, exchange(): return lax.all_to_all(x, axis, 0, 0, tiled=True)  159 us
    all_gather x2, blocking collectives, backward(): own = lax.all_gather(u_piece, 'z')  56.2 us
    ppermute x2, starting transfers between devices, backward(): other = lax.ppermute(own, 'core', swap)  20.5 us
    ppermute x2, starting transfers between devices, forward(): return exchange(mine + lax.ppermute(theirs, 'core', swap), 'z')  10.3 us
    pallas_call x2, Pallas kernels, forward(): call(forward_kernel, 'apply_plain', specs, (wide, wide), scratch)  7.39 us
  transfers between devices with their start and end apart: 4, of which 4 were waited for; matrix products, arithmetic and copies ran while one was open for 0% of the time, Pallas kernels for 0%

profile of v1, /device:TPU:1, one launch (start us, length us, event | category | flops | bytes accessed | tf_op | source)
XLA Modules:
  0.0 275.1 jit_solution(17544006919480507048)
XLA Ops:
  0.0 32.0 %all-gather = f32[16,1,64,128]{3,2,1,0:T(8,128)S(1)} all-gather(f32[1,1,64,128]{3,2,1,0:T(8,128)} %param.9), channel_id=2, replica_groups=mesh['row'=16,'z'=16,'core'=2] {'z'}, dimensions={0}, use_global_device_ids=true | all-gather | bytes 557056 | tf_op jit(solution)/shard_map/all_gather | solution.py:188
  32.1 10.1 %collective-permute-start = (f32[16,64,128]{2,1,0:T(8,128)S(1)}, f32[16,64,128]{2,1,0:T(8,128)S(1)}, u32[]{:S(2)}, u32[]{:S(2)}) collective-permute-start(f32[16,64,128]{2,1,0:T(8,128)S(1)} %bitcast.14), channel_id=1, source_target_pairs={{0,1},{1,0},{2,3},{3,2},{4,5},{5,4},{6,7},{7,6},{8,9},{9,8},{10,11... | collective-permute-start | bytes 1572872 | tf_op jit(solution)/shard_map/ppermute | solution.py:189
  42.2 1.5 collective-permute-done.other
  43.7 2.2 copy-done
  47.9 2.0 apply_transposed.2
  49.9 18.1 %all_to_all.43.got = f32[16,72,128]{2,1,0:T(8,128)S(1)} all-to-all(f32[16,72,128]{2,1,0:T(8,128)S(1)} %apply_transposed.2), channel_id=1, replica_groups=mesh['row'=16,'z'=16,'core'=2] {'row'}, dimensions={0} | all-to-all | bytes 1179648 | tf_op jit(solution)/shard_map/all_to_all | solution.py:185
  68.1 12.3 %all_to_all.44.vec = f32[16,64,128]{2,1,0:T(8,128)S(1)} all-to-all(f32[16,64,128]{2,1,0:T(8,128)S(1)} %get-tuple-element.19), channel_id=1, replica_groups=mesh['row'=16,'z'=16,'core'=2] {'row'}, dimensions={0} | all-to-all | bytes 1048576 | tf_op jit(solution)/shard_map/all_to_all | solution.py:185
  80.4 3.7 %apply_plain.2 = (f32[16,72,128]{2,1,0:T(8,128)S(1)}, f32[16,72,128]{2,1,0:T(8,128)S(1)}) custom-call(s32[64]{0:T(128)S(1)} %bitcast.20, s32[64]{0:T(128)S(1)} %bitcast.24, s32[64]{0:T(128)S(1)} %bitcast.28, s32[1]{0:T(128)} %bitcast.3.core, f32[64,128,128]{2,1,0:T(8,128)S(1)} %bitcast.11, f32[16,64,128]{2,1,0:T(8,128)S(1)} %all_to_all.44.vec), custom_call_target="tpu_custom_call" | custom-call | tf_op jit(solution)/shard_map/apply_plain/pallas_call | solution.py:199
  84.1 5.2 %collective-permute-start.1 = (f32[16,72,128]{2,1,0:T(8,128)S(1)}, f32[16,72,128]{2,1,0:T(8,128)S(1)}, u32[]{:S(2)}, u32[]{:S(2)}) collective-permute-start(f32[16,72,128]{2,1,0:T(8,128)S(1)} %get-tuple-element.21), channel_id=1, source_target_pairs={{0,1},{1,0},{2,3},{3,2},{4,5},{5,4},{6,7},{7,6},{8,9},{9,8},{10,11... | collective-permute-start | bytes 1769480 | tf_op jit(solution)/shard_map/ppermute | solution.py:200
  89.3 1.6 collective-permute-done.1
  91.0 39.6 %all_to_all.45.got = f32[16,72,128]{2,1,0:T(8,128)S(1)} all-to-all(f32[16,72,128]{2,1,0:T(8,128)S(1)} %add.18), channel_id=1, replica_groups=mesh['row'=16,'z'=16,'core'=2] {'z'}, dimensions={0} | all-to-all | bytes 1179648 | tf_op jit(solution)/shard_map/all_to_all | solution.py:185
  131.4 24.1 %all-gather.1 = f32[1024,128]{1,0:T(8,128)S(1)} all-gather(f32[64,128]{1,0:T(8,128)S(1)} %get-tuple-element.24.old), channel_id=3, replica_groups=mesh['row'=16,'z'=16,'core'=2] {'z'}, dimensions={0}, use_global_device_ids=true | all-gather | bytes 557056 | tf_op jit(solution)/shard_map/all_gather | solution.py:188
  155.5 10.3 %collective-permute-start.2 = (f32[16,64,128]{2,1,0:T(8,128)S(1)}, f32[16,64,128]{2,1,0:T(8,128)S(1)}, u32[]{:S(2)}, u32[]{:S(2)}) collective-permute-start(f32[16,64,128]{2,1,0:T(8,128)S(1)} %bitcast.16), channel_id=1, source_target_pairs={{0,1},{1,0},{2,3},{3,2},{4,5},{5,4},{6,7},{7,6},{8,9},{9,8},{10,11... | collective-permute-start | bytes 1572872 | tf_op jit(solution)/shard_map/ppermute | solution.py:189
  165.8 1.5 collective-permute-done.2.other
  167.3 2.0 apply_transposed.3
  169.3 14.5 %all_to_all.46.got = f32[16,72,128]{2,1,0:T(8,128)S(1)} all-to-all(f32[16,72,128]{2,1,0:T(8,128)S(1)} %apply_transposed.3), channel_id=1, replica_groups=mesh['row'=16,'z'=16,'core'=2] {'row'}, dimensions={0} | all-to-all | bytes 1179648 | tf_op jit(solution)/shard_map/all_to_all | solution.py:185
  184.0 12.3 %all_to_all.47.vec = f32[16,64,128]{2,1,0:T(8,128)S(1)} all-to-all(f32[16,64,128]{2,1,0:T(8,128)S(1)} %get-tuple-element.27), channel_id=1, replica_groups=mesh['row'=16,'z'=16,'core'=2] {'row'}, dimensions={0} | all-to-all | bytes 1048576 | tf_op jit(solution)/shard_map/all_to_all | solution.py:185
  196.2 3.7 %apply_plain.3 = (f32[16,72,128]{2,1,0:T(8,128)S(1)}, f32[16,72,128]{2,1,0:T(8,128)S(1)}) custom-call(s32[64]{0:T(128)S(1)} %bitcast.22, s32[64]{0:T(128)S(1)} %bitcast.26, s32[64]{0:T(128)S(1)} %bitcast.30, s32[1]{0:T(128)} %bitcast.3.core, f32[64,128,128]{2,1,0:T(8,128)S(1)} %bitcast.13, f32[16,64,128]{2,1,0:T(8,128)S(1)} %all_to_all.47.vec), custom_call_target="tpu_custom_call" | custom-call | tf_op jit(solution)/shard_map/apply_plain/pallas_call | solution.py:199
  199.9 5.2 %collective-permute-start.3 = (f32[16,72,128]{2,1,0:T(8,128)S(1)}, f32[16,72,128]{2,1,0:T(8,128)S(1)}, u32[]{:S(2)}, u32[]{:S(2)}) collective-permute-start(f32[16,72,128]{2,1,0:T(8,128)S(1)} %get-tuple-element.29), channel_id=1, source_target_pairs={{0,1},{1,0},{2,3},{3,2},{4,5},{5,4},{6,7},{7,6},{8,9},{9,8},{10,11... | collective-permute-start | bytes 1769480 | tf_op jit(solution)/shard_map/ppermute | solution.py:200
  205.1 1.6 collective-permute-done.3
  206.8 38.4 %all_to_all.48.got = f32[16,72,128]{2,1,0:T(8,128)S(1)} all-to-all(f32[16,72,128]{2,1,0:T(8,128)S(1)} %add.20), channel_id=1, replica_groups=mesh['row'=16,'z'=16,'core'=2] {'z'}, dimensions={0} | all-to-all | bytes 1179648 | tf_op jit(solution)/shard_map/all_to_all | solution.py:185
  245.9 4.3 %psum.6 = f32[8,128]{1,0:T(8,128)S(1)} all-reduce(f32[8,128]{1,0:T(8,128)S(1)} %get-tuple-element.31), channel_id=1, replica_groups=mesh['row'=16,'z'=16,'core'=2] {'core'}, use_global_device_ids=true, to_apply=%region_0.0 | all-reduce | flops 1024 | bytes 8192 | tf_op jit(solution)/shard_map/psum | solution.py:203
  250.3 14.5 %all_to_all.49 = f32[16,8,128]{2,1,0:T(8,128)S(1)} all-to-all(f32[16,8,128]{2,1,0:T(8,128)S(1)} %broadcast_in_dim.6), channel_id=1, replica_groups=mesh['row'=16,'z'=16,'core'=2] {'z'}, dimensions={0} | all-to-all | bytes 131072 | tf_op jit(solution)/shard_map/all_to_all | solution.py:185
  264.8 9.5 %all_to_all.50.got = f32[16,8,128]{2,1,0:T(8,128)S(1)} all-to-all(f32[16,8,128]{2,1,0:T(8,128)S(1)} %broadcast_in_dim.7), channel_id=1, replica_groups=mesh['row'=16,'z'=16,'core'=2] {'row'}, dimensions={0} | all-to-all | bytes 131072 | tf_op jit(solution)/shard_map/all_to_all | solution.py:185
  (28 shorter events, 4.8 us)
Async XLA Ops:
  32.1 11.7 %collective-permute-start = (f32[16,64,128]{2,1,0:T(8,128)S(1)}, f32[16,64,128]{2,1,0:T(8,128)S(1)}, u32[]{:S(2)}, u32[]{:S(2)}) collective-permute-start(f32[16,64,128]{2,1,0:T(8,128)S(1)} %bitcast.14), channel_id=1, source_target_pairs={{0,1},{1,0},{2,3},{3,2},{4,5},{5,4},{6,7},{7,6},{8,9},{9,8},{10,11... | collective-permute-start | bytes 1572872 | tf_op jit(solution)/shard_map/ppermute | solution.py:189
  43.7 2.2 copy-start
  45.9 0.7 copy-start.3
  46.6 0.7 copy-start.5
  47.2 0.7 copy-start.7
  47.9 32.5 %copy-start.1 = (f32[1,1,64,128,128]{4,3,2,1,0:T(8,128)S(1)}, f32[1,1,64,128,128]{4,3,2,1,0:T(8,128)}, u32[]{:S(2)}) copy-start(f32[1,1,64,128,128]{4,3,2,1,0:T(8,128)} %param.5) | copy-start | bytes 12582916
  47.9 32.5 %copy-start.4 = (s32[1,1,64]{2,1,0:T(1,128)S(1)}, s32[1,1,64]{2,1,0:T(1,128)}, u32[]{:S(2)}) copy-start(s32[1,1,64]{2,1,0:T(1,128)} %param.6) | copy-start | bytes 772
  47.9 32.5 %copy-start.6 = (s32[1,1,64]{2,1,0:T(1,128)S(1)}, s32[1,1,64]{2,1,0:T(1,128)}, u32[]{:S(2)}) copy-start(s32[1,1,64]{2,1,0:T(1,128)} %param.7) | copy-start | bytes 772
  47.9 32.5 %copy-start.8 = (s32[1,1,64]{2,1,0:T(1,128)S(1)}, s32[1,1,64]{2,1,0:T(1,128)}, u32[]{:S(2)}) copy-start(s32[1,1,64]{2,1,0:T(1,128)} %param.8) | copy-start | bytes 772
  68.1 62.4 %copy-start.2 = (f32[1,1,64,128]{3,2,1,0:T(8,128)S(1)}, f32[1,1,64,128]{3,2,1,0:T(8,128)}, u32[]{:S(2)}) copy-start(f32[1,1,64,128]{3,2,1,0:T(8,128)} %param.9) | copy-start | bytes 98308
  84.1 6.8 %collective-permute-start.1 = (f32[16,72,128]{2,1,0:T(8,128)S(1)}, f32[16,72,128]{2,1,0:T(8,128)S(1)}, u32[]{:S(2)}, u32[]{:S(2)}) collective-permute-start(f32[16,72,128]{2,1,0:T(8,128)S(1)} %get-tuple-element.21), channel_id=1, source_target_pairs={{0,1},{1,0},{2,3},{3,2},{4,5},{5,4},{6,7},{7,6},{8,9},{9,8},{10,11... | collective-permute-start | bytes 1769480 | tf_op jit(solution)/shard_map/ppermute | solution.py:200
  155.5 11.8 %collective-permute-start.2 = (f32[16,64,128]{2,1,0:T(8,128)S(1)}, f32[16,64,128]{2,1,0:T(8,128)S(1)}, u32[]{:S(2)}, u32[]{:S(2)}) collective-permute-start(f32[16,64,128]{2,1,0:T(8,128)S(1)} %bitcast.16), channel_id=1, source_target_pairs={{0,1},{1,0},{2,3},{3,2},{4,5},{5,4},{6,7},{7,6},{8,9},{9,8},{10,11... | collective-permute-start | bytes 1572872 | tf_op jit(solution)/shard_map/ppermute | solution.py:189
  199.9 6.8 %collective-permute-start.3 = (f32[16,72,128]{2,1,0:T(8,128)S(1)}, f32[16,72,128]{2,1,0:T(8,128)S(1)}, u32[]{:S(2)}, u32[]{:S(2)}) collective-permute-start(f32[16,72,128]{2,1,0:T(8,128)S(1)} %get-tuple-element.29), channel_id=1, source_target_pairs={{0,1},{1,0},{2,3},{3,2},{4,5},{5,4},{6,7},{7,6},{8,9},{9,8},{10,11... | collective-permute-start | bytes 1769480 | tf_op jit(solution)/shard_map/ppermute | solution.py:200

commit v2 on v1

v2 whole, which is shorter than its diff:
```python
import jax
import jax.numpy as jnp
from jax import lax
from jax.experimental import pallas as pl
from jax.experimental.pallas import tpu as pltpu
from jax.sharding import Mesh, PartitionSpec as P

W = 128
SLOTS = 64
UNROLL = 32
GROUP = 16
HALF = 32
RBL = 32
CBL = 16
NZ = 16
ROWS = 16
ITERS = 2
PAD = 8
eps = 1e-06
SCALE = 0.25
TINY = 2.0**-64
LARGE = 1e37

F32 = jnp.float32
BF16 = jnp.bfloat16

SMEM = pl.BlockSpec(memory_space=pltpu.SMEM)
VMEM = pl.BlockSpec(memory_space=pltpu.VMEM)
ANY = pl.BlockSpec(memory_space=pl.ANY)
PARAMS = pltpu.CompilerParams(vmem_limit_bytes=36 << 20)


def root(total):
    return jnp.sqrt(total + eps)


def halves(x):
    hi = x.astype(BF16)
    return hi, (x - hi.astype(F32)).astype(BF16)


def diagonal(count):
    shape = (count, W)
    return lax.broadcasted_iota(jnp.int32, shape, 0) == lax.broadcasted_iota(jnp.int32, shape, 1)


def to_row(col):
    return jnp.sum(jnp.where(diagonal(col.shape[0]), col, 0.0), axis=0, keepdims=True)


def to_col(row, count):
    return jnp.sum(jnp.where(diagonal(count), row, 0.0), axis=1, keepdims=True)


def spread(col):
    return jnp.broadcast_to(col, (col.shape[0], W))


def per_vector(squares):
    total = jnp.sum(squares, axis=1, keepdims=True)
    total = total[:HALF] + total[HALF:]
    return jnp.concatenate([total, total], axis=0)


def norm_rows(squares):
    return jnp.broadcast_to(to_row(per_vector(squares)), (PAD, W))


def add_product(slots, s, side, high, low, parts, acc, source, target, unused):
    vec = parts[source(side, slots, s)]
    prod = jnp.dot(vec, jnp.concatenate([high, high], axis=0), preferred_element_type=F32)
    prod += jnp.dot(vec[:, :W], low, preferred_element_type=F32)
    acc[jnp.where(slots[2, s] > 0, target(side, slots, s), unused)] += prod


def products(sides, parts, acc, source, target, unused):
    acc[...] = jnp.zeros_like(acc)
    for side, (slots, hi, lo) in enumerate(sides):

        def group(index, carry):
            for offset in range(UNROLL):
                s = index * UNROLL + offset
                add_product(slots, s, side, hi[s], lo[s], parts, acc, source, target, unused)
            return carry

        lax.fori_loop(0, SLOTS // UNROLL, group, 0)


def by_row(side, slots, s):
    return slots[0, s]


def by_col(side, slots, s):
    return slots[1, s] + side * CBL


def store_tiles(parts, first, second, x):
    both = jnp.concatenate(halves(x * SCALE), axis=1)
    parts[first] = both[:HALF]
    parts[second] = both[HALF:]


def emit_cols(out, acc, squares):
    norms = norm_rows(squares)
    for c in range(CBL):
        out[c, :HALF] = acc[c]
        out[c, HALF : 2 * HALF] = acc[CBL + c]
        out[c, 2 * HALF :] = norms


def first_backward_kernel(slots0, slots1, mats0, mats1, vec, out, *rest):
    kept, (blocks, arrived, parts, acc) = rest[:8], rest[8:]
    groups = SLOTS // GROUP
    copies = []
    for side, mats in enumerate((mats0, mats1)):
        for index in range(groups):
            some = pl.ds(index * GROUP, GROUP)
            where = side * groups + index
            copies.append(pltpu.make_async_copy(mats.at[some], blocks.at[side, some], arrived.at[where]))
    for copy in copies:
        copy.start()
    squares = jnp.zeros((2 * HALF, W), F32)
    for z in range(NZ):
        x = vec[z]
        squares += x * x
        store_tiles(parts, 2 * z, 2 * z + 1, x)
    acc[...] = jnp.zeros_like(acc)
    for side, slots in enumerate((slots0, slots1)):
        hi, lo, hi_t, lo_t = kept[4 * side : 4 * side + 4]
        for index in range(groups):
            copies[side * groups + index].wait()
            for s in range(index * GROUP, (index + 1) * GROUP):
                block = blocks[side, s]
                high, low = halves(block)
                hi[s], lo[s] = high, low
                hi_t[s], lo_t[s] = halves(block.T)
                add_product(slots, s, side, high, low, parts, acc, by_row, by_col, 2 * CBL)
    emit_cols(out, acc, squares)


def backward_kernel(slots0, slots1, hi0, lo0, hi1, lo1, vec, out, scale, factor, parts, acc):
    count = 2 * HALF
    total = jnp.zeros((PAD, W), F32)
    for z in range(NZ):
        total += vec[z, count:]
    alpha = root(to_col(total[:1], count))
    scale[...] = spread(alpha)
    inverse = spread(1.0 / (SCALE * alpha))
    factor[...] = inverse
    squares = jnp.zeros((count, W), F32)
    for z in range(NZ):
        x = vec[z, :count] * inverse
        squares += x * x
        store_tiles(parts, 2 * z, 2 * z + 1, x)
    sides = ((slots0, hi0, lo0), (slots1, hi1, lo1))
    products(sides, parts, acc, by_row, by_col, 2 * CBL)
    emit_cols(out, acc, squares)


def forward_kernel(slots0, slots1, hi0, lo0, hi1, lo1, vec, old, first, second, out, norms, parts, acc):
    count = 2 * HALF
    squares = jnp.zeros((count, W), F32)
    for c in range(CBL):
        x = vec[c]
        squares += x * x
        store_tiles(parts, c, CBL + c, x)
    sides = ((slots0, hi0, lo0), (slots1, hi1, lo1))
    products(sides, parts, acc, by_col, by_row, RBL)
    norms[...] = norm_rows(squares)
    weight = SCALE * spread(per_vector(squares))
    for z in range(NZ):
        less = weight * ((old[z, :count] * first[...]) * second[...])
        out[z, :HALF] = acc[2 * z] - less[:HALF]
        out[z, HALF:] = acc[2 * z + 1] - less[HALF:]


def summed(got):
    total = got[0]
    for index in range(1, got.shape[0]):
        total += got[index]
    return total


def first_cols_kernel(got, copies, fresh, scale, inverse):
    count = fresh.shape[0]
    total = summed(got)
    beta = root(to_col(total[count : count + 1], count))
    vec = total[:count] / (SCALE * beta)
    fresh[...] = vec
    copies[...] = jnp.broadcast_to(vec[None], copies.shape)
    scale[...] = spread(beta)
    inverse[...] = spread(1.0 / beta)


def cols_kernel(got, old, alpha, copies, fresh, scale, inverse):
    count = fresh.shape[0]
    total = summed(got)
    beta = root(to_col(total[count : count + 1], count))
    vec = total[:count] / (SCALE * beta) - beta * (old[...] / alpha[...])
    fresh[...] = vec
    copies[...] = jnp.broadcast_to(vec[None], copies.shape)
    scale[...] = spread(beta)
    inverse[...] = spread(1.0 / beta)


def rows_kernel(got, old, first, second, norms, fresh):
    count = first.shape[0]
    fresh[:count] = summed(got) - (SCALE * eps) * ((old[:count] * first[...]) * second[...])
    fresh[count:] = norms[...]


def lanes(start):
    shape = (2 * HALF, W)
    vector = lax.rem(lax.broadcasted_iota(jnp.int32, shape, 0), HALF)
    return lax.broadcasted_iota(jnp.int32, shape, 1) == vector + start


def row_at(squares, start):
    return jnp.sum(jnp.where(lanes(start), jnp.sum(squares, axis=1, keepdims=True), 0.0), axis=0, keepdims=True)


def col_at(row, start):
    return jnp.sum(jnp.where(lanes(start), row, 0.0), axis=1, keepdims=True)


def squares_kernel(piece, out):
    count = 2 * HALF
    vec = piece[:count]
    small = vec * TINY
    norms = col_at(piece[count : count + 1], 0) * (0.5 / ROWS)
    norms = jnp.sum(jnp.where(lanes(2 * HALF), norms, 0.0), axis=0, keepdims=True)
    out[...] = row_at(vec * vec, 0) + row_at(small * small, HALF) + norms


def last_kernel(got, scale_alpha, scale_beta):
    total = got[...]
    alpha = root(col_at(total, 2 * HALF))
    plain, small = col_at(total, 0), col_at(total, HALF)
    norm = jnp.where(plain < LARGE, jnp.sqrt(plain), jnp.sqrt(small) / TINY)
    norm = norm / (SCALE * alpha)
    scale_alpha[...] = spread(alpha)
    scale_beta[...] = spread(root(norm * norm))


def total_kernel(got, scale):
    scale[...] = spread(root(col_at(got[...], 0)))


def call(kernel, name, specs, outs, scratch=()):
    return pl.pallas_call(
        kernel,
        out_shape=outs,
        in_specs=specs,
        out_specs=jax.tree.map(lambda _: VMEM, outs),
        scratch_shapes=scratch,
        compiler_params=PARAMS,
        name=name,
    )


def array(*shape):
    return jax.ShapeDtypeStruct(shape, F32)


def advance(state, vec, alpha, beta):
    x_vec, w_vec, phibar, rhobar = state
    rho = jnp.sqrt(rhobar * rhobar + beta * beta)
    cosine = rhobar / rho
    sine = beta / rho
    theta = sine * alpha
    rhobar = -cosine * alpha
    phi = cosine * phibar
    phibar = sine * phibar
    x_vec = x_vec + (phi / rho) * w_vec
    w_vec = vec - (theta / rho) * w_vec
    return (x_vec, w_vec, phibar, rhobar)


def on_device(blocks, block_rows, block_cols, block_valid, rhs):
    mats = blocks[0, 0]
    me = lax.axis_index("core")
    swap = [(0, 1), (1, 0)]
    count = 2 * HALF
    tile, rows_tile = array(count, W), array(PAD, W)
    copied, wide = array(CBL, count, W), array(CBL, count + PAD, W)
    halved = jax.ShapeDtypeStruct(mats.shape, BF16)

    def exchange(x, axis):
        return lax.all_to_all(x, axis, 0, 0, tiled=True)

    def other_core(x):
        return lax.ppermute(x, "core", swap)

    def in_order(mine, other):
        return jnp.concatenate([jnp.where(me == 0, mine, other), jnp.where(me == 0, other, mine)])

    def scratch(sources, targets):
        return (pltpu.VMEM((sources, HALF, 2 * W), BF16), pltpu.VMEM((targets + 1, HALF, W), F32))

    pieces = rhs[0, 0].reshape(2, HALF, W)
    mine = jnp.where(me == 0, pieces[0], pieces[1])
    rest = jnp.where(me == 0, pieces[1], pieces[0])
    own_slots = jnp.stack([block_rows[0, 0], block_cols[0, 0], block_valid[0, 0]])
    listed = jnp.pad(own_slots.astype(F32), ((0, PAD - 3), (0, W - SLOTS)))
    got = other_core(jnp.concatenate([rest, listed]))
    slots = (own_slots, got[HALF : HALF + 3, :SLOTS].astype(jnp.int32))
    piece = in_order(mine, got[:HALF])
    other_mats, _ = lax.optimization_barrier((mats, got))
    other_mats = other_core(other_mats)
    specs = [SMEM] * 2 + [VMEM] * 5

    def first_backward():
        full = lax.all_gather(piece, "z")
        outs = (wide,) + (halved,) * 8
        held = (pltpu.VMEM((2, SLOTS, W, W), F32), pltpu.SemaphoreType.DMA((2 * SLOTS // GROUP,)))
        in_specs = [SMEM] * 2 + [ANY] * 2 + [VMEM]
        apply = call(first_backward_kernel, "apply_first", in_specs, outs, held + scratch(RBL, 2 * CBL))
        part, hi0, lo0, hi_t0, lo_t0, hi1, lo1, hi_t1, lo_t1 = apply(*slots, mats, other_mats, full)
        return exchange(part, "row"), full, (hi0, lo0, hi1, lo1), (hi_t0, lo_t0, hi_t1, lo_t1)

    def backward(fresh):
        full = lax.all_gather(fresh, "z")
        apply = call(backward_kernel, "apply_transposed", specs, (wide, tile, tile), scratch(RBL, 2 * CBL))
        part, alpha, factor = apply(*slots, *plain, full)
        return exchange(part, "row"), full, alpha, factor

    def forward(copies, full, first, second):
        vec = exchange(copies, "row")
        apply = call(
            forward_kernel, "apply_plain", specs + [VMEM] * 3, (copied, rows_tile), scratch(2 * CBL, RBL)
        )
        part, norms = apply(*slots, *turned, vec, full, first, second)
        return exchange(part, "z"), norms

    def everywhere(row):
        copies = jnp.broadcast_to(row[None], (ROWS * NZ, 1, W))
        return jnp.sum(exchange(copies, ("row", "z")), axis=0)

    got, full, plain, turned = first_backward()
    outs = (copied, tile, tile, tile)
    copies, v_old, beta, second = call(first_cols_kernel, "first_cols", [VMEM], outs)(got)
    u_old, first = piece, jnp.ones((count, W), F32)
    state = None
    for step_index in range(ITERS):
        got, norms = forward(copies, full, first, second)
        fresh = call(rows_kernel, "rows", [VMEM] * 5, array(count + PAD, W))(got, u_old, first, second, norms)
        got, full, alpha, first = backward(fresh)
        u_old = fresh
        if step_index == ITERS - 1:
            last = everywhere(call(squares_kernel, "squares", [VMEM], array(1, W))(fresh))
            alpha, last_beta = call(last_kernel, "last", [VMEM], (tile, tile))(last)
        v_now = v_old / alpha
        if state is None:
            state = (jnp.zeros_like(v_now), v_now, beta, alpha)
        else:
            state = advance(state, v_now, alpha, beta)
        copies, v_old, beta, second = call(cols_kernel, "cols", [VMEM] * 3, outs)(got, v_old, alpha)
    squares = jnp.sum(v_old * v_old, axis=1)
    squares = squares[:HALF] + squares[HALF:]
    total = everywhere(jnp.pad(squares, (0, W - HALF))[None])
    alpha = call(total_kernel, "total", [VMEM], tile)(total)
    x_vec = advance(state, v_old / alpha, alpha, last_beta)[0]
    return in_order(x_vec[:HALF], other_core(x_vec[HALF:]))[None, None]


def solution(mesh):
    grid = Mesh(mesh.devices.reshape(16, NZ, 2), ("row", "z", "core"))
    col = ("z", "core")
    placed = (
        P("row", col, None, None, None),
        P("row", col, None),
        P("row", col, None),
        P("row", col, None),
        P("row", col, None, None),
    )
    return jax.shard_map(
        on_device,
        mesh=grid,
        in_specs=placed,
        out_specs=P("row", col, None, None),
        check_vma=False,
    )
```

time: 277 us -> 244 us (0.88)
  blocking collectives: 220 us -> 184 us
  starting transfers between devices: 30.8 us -> 35.5 us
  waiting for transfers between devices: 6.24 us -> 1.64 us
  Pallas kernels: 13.3 us -> 16.9 us
    all_to_all x8 -> x7, blocking collectives: 159 us -> 129 us  [exchange(): return lax.all_to_all(x, axis, 0, 0, tiled=True)]
    ppermute x4 -> x3, starting transfers between devices: 30.8 us -> 35.5 us  [other_core(): return lax.ppermute(x, 'core', swap)]
    ppermute x4 -> x3, waiting for transfers between devices: 6.24 us -> 1.64 us  [other_core(): return lax.ppermute(x, 'core', swap)]
    psum x1 -> x0, blocking collectives: 4.31 us -> none  [everywhere(): norms = lax.psum(norms, 'core')]
    pallas_call x9 -> x10, Pallas kernels: 13.3 us -> 16.9 us  [the longest x2 7.24 us: forward(): part, norms = apply(*slots, *turned, vec, full, first, second)]
  transfers between devices with their start and end apart: 4 -> 3, of which waited for: 4 -> 2; matrix products, arithmetic and copies ran while one was open for 0% -> 0% of each run, Pallas kernels for 0% -> 0%
where the time goes in v2:
time: 244 us; the launch traced here: 243 us
  blocking collectives  184 us (75%)
  starting transfers between devices  35.5 us (15%)
  Pallas kernels  16.9 us (7%)
  other arithmetic  2.94 us (1%)
    all_to_all x7, blocking collectives, exchange(): return lax.all_to_all(x, axis, 0, 0, tiled=True)  129 us
    ppermute x3, starting transfers between devices, other_core(): return lax.ppermute(x, 'core', swap)  35.5 us
    all_gather x1, blocking collectives, backward(): full = lax.all_gather(fresh, 'z')  28 us
    all_gather x1, blocking collectives, first_backward(): full = lax.all_gather(piece, 'z')  26.2 us
    pallas_call x2, Pallas kernels, forward(): part, norms = apply(*slots, *turned, vec, full, first, second)  7.24 us
    pallas_call x1, Pallas kernels, first_backward(): apply(*slots, mats, other_mats, full)  5.4 us
  transfers between devices with their start and end apart: 3, of which 2 were waited for; matrix products, arithmetic and copies ran while one was open for 0% of the time, Pallas kernels for 0%

profile of v2, /device:TPU:1, one launch (start us, length us, event | category | flops | bytes accessed | tf_op | source)
XLA Modules:
  0.0 242.8 jit_solution(11318579653936367686)
XLA Ops:
  0.0 0.7 select_bitcast_fusion
  0.7 0.7 fusion
  1.4 8.8 %collective-permute-start = (f32[40,128]{1,0:T(8,128)S(1)}, f32[40,128]{1,0:T(8,128)S(1)}, u32[]{:S(2)}, u32[]{:S(2)}) collective-permute-start(f32[40,128]{1,0:T(8,128)S(1)} %select_maximum_fusion), channel_id=1, source_target_pairs={{0,1},{1,0},{2,3},{3,2},{4,5},{5,4},{6,7},{7,6},{8,9},{9,8},{10,11... | collective-permute-start | bytes 61448 | tf_op jit(solution)/shard_map/ppermute | solution.py:292
  10.2 0.8 collective-permute-done
  11.1 2.2 collective-permute-start.1
  13.3 0.7 bitcast_select_fusion.1
  14.1 26.2 %all-gather = f32[1024,128]{1,0:T(8,128)S(1)} all-gather(f32[64,128]{1,0:T(8,128)S(1)} %pad_maximum_fusion.old), channel_id=2, replica_groups=mesh['row'=16,'z'=16,'core'=2] {'z'}, dimensions={0}, use_global_device_ids=true | all-gather | bytes 557056 | tf_op jit(solution)/shard_map/all_gather | solution.py:313
  40.3 2.0 copy-done
  42.2 5.4 %apply_first.1 = (f32[16,72,128]{2,1,0:T(8,128)S(1)}, bf16[64,128,128]{2,1,0:T(8,128)(2,1)S(1)}, bf16[64,128,128]{2,1,0:T(8,128)(2,1)S(1)}, bf16[64,128,128]{2,1...) custom-call(s32[3,64]{1,0:T(4,128)S(1)} %get-tuple-element.64.slots0, ...), custom_call_target="tpu_custom_call" | custom-call | tf_op jit(solution)/shard_map/apply_first/pallas_call | solution.py:318
  47.6 15.9 %all_to_all.37.got = f32[16,72,128]{2,1,0:T(8,128)S(1)} all-to-all(f32[16,72,128]{2,1,0:T(8,128)S(1)} %get-tuple-element.41), channel_id=1, replica_groups=mesh['row'=16,'z'=16,'core'=2] {'row'}, dimensions={0} | all-to-all | bytes 1179648 | tf_op jit(solution)/shard_map/all_to_all | solution.py:289
  63.7 11.9 %all_to_all.38.vec = f32[16,64,128]{2,1,0:T(8,128)S(1)} all-to-all(f32[16,64,128]{2,1,0:T(8,128)S(1)} %get-tuple-element.42), channel_id=1, replica_groups=mesh['row'=16,'z'=16,'core'=2] {'row'}, dimensions={0} | all-to-all | bytes 1048576 | tf_op jit(solution)/shard_map/all_to_all | solution.py:289
  75.6 3.6 %apply_plain.2 = (f32[16,64,128]{2,1,0:T(8,128)S(1)}, f32[8,128]{1,0:T(8,128)S(1)}) custom-call(s32[3,64]{1,0:T(4,128)S(1)} %get-tuple-element.64.slots0, s32[3,64]{1,0:T(4,128)S(1)} %slice_convert_fusion.slots1, bf16[64,128,128]{2,1,0:T(8,128)(2,1)S(1)} %get-tuple-element.37.hi0, bf16[64,128,128]{2,1,0:T(8,128)(2,1)S(1)} %get-tuple-element.38.lo0, ...), custom_call_target="tpu_custom_call" | custom-call | tf_op jit(solution)/shard_map/apply_plain/pallas_call | solution.py:332
  79.2 23.0 %all_to_all.39.got = f32[16,64,128]{2,1,0:T(8,128)S(1)} all-to-all(f32[16,64,128]{2,1,0:T(8,128)S(1)} %get-tuple-element.44), channel_id=1, replica_groups=mesh['row'=16,'z'=16,'core'=2] {'z'}, dimensions={0} | all-to-all | bytes 1048576 | tf_op jit(solution)/shard_map/all_to_all | solution.py:289
  102.2 28.0 %all-gather.1 = f32[1152,128]{1,0:T(8,128)S(1)} all-gather(f32[72,128]{1,0:T(8,128)S(1)} %rows.2.old), channel_id=3, replica_groups=mesh['row'=16,'z'=16,'core'=2] {'z'}, dimensions={0}, use_global_device_ids=true | all-gather | bytes 626688 | tf_op jit(solution)/shard_map/all_gather | solution.py:322
  130.2 3.7 %apply_transposed.1 = (f32[16,72,128]{2,1,0:T(8,128)S(1)}, f32[64,128]{1,0:T(8,128)S(1)}, f32[64,128]{1,0:T(8,128)S(1)}) custom-call(s32[3,64]{1,0:T(4,128)S(1)} %get-tuple-element.64.slots0, s32[3,64]{1,0:T(4,128)S(1)} %slice_convert_fusion.slots1, bf16[64,128,128]{2,1,0:T(8,128)(2,1)S(1)} %get-tuple-element.33.hi0, ...), custom_call_target="tpu_custom_call" | custom-call | tf_op jit(solution)/shard_map/apply_transposed/pallas_call | solution.py:324
  133.9 12.3 %all_to_all.40.got = f32[16,72,128]{2,1,0:T(8,128)S(1)} all-to-all(f32[16,72,128]{2,1,0:T(8,128)S(1)} %get-tuple-element.47), channel_id=1, replica_groups=mesh['row'=16,'z'=16,'core'=2] {'row'}, dimensions={0} | all-to-all | bytes 1179648 | tf_op jit(solution)/shard_map/all_to_all | solution.py:289
  146.2 0.2 cols.1
  146.3 11.9 %all_to_all.41.vec = f32[16,64,128]{2,1,0:T(8,128)S(1)} all-to-all(f32[16,64,128]{2,1,0:T(8,128)S(1)} %get-tuple-element.51), channel_id=1, replica_groups=mesh['row'=16,'z'=16,'core'=2] {'row'}, dimensions={0} | all-to-all | bytes 1048576 | tf_op jit(solution)/shard_map/all_to_all | solution.py:289
  158.2 3.6 %apply_plain.3 = (f32[16,64,128]{2,1,0:T(8,128)S(1)}, f32[8,128]{1,0:T(8,128)S(1)}) custom-call(s32[3,64]{1,0:T(4,128)S(1)} %get-tuple-element.64.slots0, s32[3,64]{1,0:T(4,128)S(1)} %slice_convert_fusion.slots1, bf16[64,128,128]{2,1,0:T(8,128)(2,1)S(1)} %get-tuple-element.37.hi0, bf16[64,128,128]{2,1,0:T(8,128)(2,1)S(1)} %get-tuple-element.38.lo0, ...), custom_call_target="tpu_custom_call" | custom-call | tf_op jit(solution)/shard_map/apply_plain/pallas_call | solution.py:332
  161.9 25.1 %all_to_all.42.got = f32[16,64,128]{2,1,0:T(8,128)S(1)} all-to-all(f32[16,64,128]{2,1,0:T(8,128)S(1)} %get-tuple-element.54), channel_id=1, replica_groups=mesh['row'=16,'z'=16,'core'=2] {'z'}, dimensions={0} | all-to-all | bytes 1048576 | tf_op jit(solution)/shard_map/all_to_all | solution.py:289
  187.2 29.4 %all_to_all.43 = f32[256,1,128]{2,1,0:T(1,128)S(1)} all-to-all(f32[256,1,128]{2,1,0:T(1,128)S(1)} %broadcast_in_dim.19), channel_id=1, replica_groups=mesh['row'=16,'z'=16,'core'=2] {'row','z'}, dimensions={0} | all-to-all | bytes 262144 | tf_op jit(solution)/shard_map/all_to_all | solution.py:289
  216.9 24.5 %collective-permute-start.2 = (f32[32,128]{1,0:T(8,128)S(1)}, f32[32,128]{1,0:T(8,128)S(1)}, u32[]{:S(2)}, u32[]{:S(2)}) collective-permute-start(f32[32,128]{1,0:T(8,128)S(1)} %slice.33), channel_id=1, source_target_pairs={{0,1},{1,0},{2,3},{3,2},{4,5},{5,4},{6,7},{7,6},{8,9},{9,8},{10,11... | collective-permute-start | bytes 49160 | tf_op jit(solution)/shard_map/ppermute | solution.py:292
  241.4 0.8 collective-permute-done.2
  242.2 0.6 maximum_bitcast_fusion
  (16 shorter events, 0.7 us)
Async XLA Ops:
  1.4 9.6 %collective-permute-start = (f32[40,128]{1,0:T(8,128)S(1)}, f32[40,128]{1,0:T(8,128)S(1)}, u32[]{:S(2)}, u32[]{:S(2)}) collective-permute-start(f32[40,128]{1,0:T(8,128)S(1)} %select_maximum_fusion), channel_id=1, source_target_pairs={{0,1},{1,0},{2,3},{3,2},{4,5},{5,4},{6,7},{7,6},{8,9},{9,8},{10,11... | collective-permute-start | bytes 61448 | tf_op jit(solution)/shard_map/ppermute | solution.py:292
  11.1 29.2 %collective-permute-start.1 = (f32[64,128,128]{2,1,0:T(8,128)}, f32[64,128,128]{2,1,0:T(8,128)S(1)}, u32[]{:S(2)}, u32[]{:S(2)}) collective-permute-start(f32[64,128,128]{2,1,0:T(8,128)} %bitcast.22), channel_id=1, source_target_pairs={{0,1},{1,0},{2,3},{3,2},{4,5},{5,4},{6,7},{7,6},{8,9},{9,8},{10,11... | collective-permute-start | bytes 12582920 | tf_op jit(solution)/shard_map/ppermute | solution.py:292
  40.3 2.0 copy-start
  216.9 25.3 %collective-permute-start.2 = (f32[32,128]{1,0:T(8,128)S(1)}, f32[32,128]{1,0:T(8,128)S(1)}, u32[]{:S(2)}, u32[]{:S(2)}) collective-permute-start(f32[32,128]{1,0:T(8,128)S(1)} %slice.33), channel_id=1, source_target_pairs={{0,1},{1,0},{2,3},{3,2},{4,5},{5,4},{6,7},{7,6},{8,9},{9,8},{10,11... | collective-permute-start | bytes 49160 | tf_op jit(solution)/shard_map/ppermute | solution.py:292

commit v3 on v2

--- a/solution.py
+++ b/solution.py
@@ -7,7 +7,6 @@
 
 W = 128
 SLOTS = 64
-UNROLL = 32
 GROUP = 16
 HALF = 32
 RBL = 32
@@ -26,8 +25,8 @@
 
 SMEM = pl.BlockSpec(memory_space=pltpu.SMEM)
 VMEM = pl.BlockSpec(memory_space=pltpu.VMEM)
-ANY = pl.BlockSpec(memory_space=pl.ANY)
-PARAMS = pltpu.CompilerParams(vmem_limit_bytes=36 << 20)
+HBM = pl.BlockSpec(memory_space=pltpu.HBM)
+PARAMS = pltpu.CompilerParams(vmem_limit_bytes=16 << 20)
 
 
 def root(total):
@@ -67,23 +66,17 @@
 
 
 def add_product(slots, s, side, high, low, parts, acc, source, target, unused):
-    vec = parts[source(side, slots, s)]
-    prod = jnp.dot(vec, jnp.concatenate([high, high], axis=0), preferred_element_type=F32)
-    prod += jnp.dot(vec[:, :W], low, preferred_element_type=F32)
+    both = jnp.concatenate([high, low], axis=1)
+    prod = jnp.dot(parts[source(side, slots, s)], both, preferred_element_type=F32)
+    prod = prod[:HALF, :W] + (prod[HALF:, :W] + prod[:HALF, W:])
     acc[jnp.where(slots[2, s] > 0, target(side, slots, s), unused)] += prod
 
 
 def products(sides, parts, acc, source, target, unused):
     acc[...] = jnp.zeros_like(acc)
     for side, (slots, hi, lo) in enumerate(sides):
-
-        def group(index, carry):
-            for offset in range(UNROLL):
-                s = index * UNROLL + offset
-                add_product(slots, s, side, hi[s], lo[s], parts, acc, source, target, unused)
-            return carry
-
-        lax.fori_loop(0, SLOTS // UNROLL, group, 0)
+        for s in range(SLOTS):
+            add_product(slots, s, side, hi[s], lo[s], parts, acc, source, target, unused)
 
 
 def by_row(side, slots, s):
@@ -95,9 +88,9 @@
 
 
 def store_tiles(parts, first, second, x):
-    both = jnp.concatenate(halves(x * SCALE), axis=1)
-    parts[first] = both[:HALF]
-    parts[second] = both[HALF:]
+    hi, lo = halves(x * SCALE)
+    parts[first] = jnp.concatenate([hi[:HALF], lo[:HALF]], axis=0)
+    parts[second] = jnp.concatenate([hi[HALF:], lo[HALF:]], axis=0)
 
 
 def emit_cols(out, acc, squares):
@@ -110,31 +103,27 @@
 
 def first_backward_kernel(slots0, slots1, mats0, mats1, vec, out, *rest):
     kept, (blocks, arrived, parts, acc) = rest[:8], rest[8:]
-    groups = SLOTS // GROUP
     copies = []
-    for side, mats in enumerate((mats0, mats1)):
-        for index in range(groups):
-            some = pl.ds(index * GROUP, GROUP)
-            where = side * groups + index
-            copies.append(pltpu.make_async_copy(mats.at[some], blocks.at[side, some], arrived.at[where]))
-    for copy in copies:
-        copy.start()
+    for index in range(SLOTS // GROUP):
+        some = pl.ds(index * GROUP, GROUP)
+        copies.append(pltpu.make_async_copy(mats0.at[some], blocks.at[some], arrived.at[index]))
+        copies[index].start()
     squares = jnp.zeros((2 * HALF, W), F32)
     for z in range(NZ):
         x = vec[z]
         squares += x * x
         store_tiles(parts, 2 * z, 2 * z + 1, x)
     acc[...] = jnp.zeros_like(acc)
-    for side, slots in enumerate((slots0, slots1)):
+    for side, slots, mats in ((1, slots1, mats1), (0, slots0, blocks)):
         hi, lo, hi_t, lo_t = kept[4 * side : 4 * side + 4]
-        for index in range(groups):
-            copies[side * groups + index].wait()
-            for s in range(index * GROUP, (index + 1) * GROUP):
-                block = blocks[side, s]
-                high, low = halves(block)
-                hi[s], lo[s] = high, low
-                hi_t[s], lo_t[s] = halves(block.T)
-                add_product(slots, s, side, high, low, parts, acc, by_row, by_col, 2 * CBL)
+        for s in range(SLOTS):
+            if side == 0 and s % GROUP == 0:
+                copies[s // GROUP].wait()
+            block = mats[s]
+            high, low = halves(block)
+            hi[s], lo[s] = high, low
+            hi_t[s], lo_t[s] = halves(block.T)
+            add_product(slots, s, side, high, low, parts, acc, by_row, by_col, 2 * CBL)
     emit_cols(out, acc, squares)
 
 
@@ -295,7 +284,7 @@
         return jnp.concatenate([jnp.where(me == 0, mine, other), jnp.where(me == 0, other, mine)])
 
     def scratch(sources, targets):
-        return (pltpu.VMEM((sources, HALF, 2 * W), BF16), pltpu.VMEM((targets + 1, HALF, W), F32))
+        return (pltpu.VMEM((sources, 2 * HALF, W), BF16), pltpu.VMEM((targets + 1, HALF, W), F32))
 
     pieces = rhs[0, 0].reshape(2, HALF, W)
     mine = jnp.where(me == 0, pieces[0], pieces[1])
@@ -312,8 +301,8 @@
     def first_backward():
         full = lax.all_gather(piece, "z")
         outs = (wide,) + (halved,) * 8
-        held = (pltpu.VMEM((2, SLOTS, W, W), F32), pltpu.SemaphoreType.DMA((2 * SLOTS // GROUP,)))
-        in_specs = [SMEM] * 2 + [ANY] * 2 + [VMEM]
+        held = (pltpu.VMEM((SLOTS, W, W), F32), pltpu.SemaphoreType.DMA((SLOTS // GROUP,)))
+        in_specs = [SMEM] * 2 + [HBM] + [VMEM] * 2
         apply = call(first_backward_kernel, "apply_first", in_specs, outs, held + scratch(RBL, 2 * CBL))
         part, hi0, lo0, hi_t0, lo_t0, hi1, lo1, hi_t1, lo_t1 = apply(*slots, mats, other_mats, full)
         return exchange(part, "row"), full, (hi0, lo0, hi1, lo1), (hi_t0, lo_t0, hi_t1, lo_t1)

time: 244 us -> 239 us (0.980)
  Pallas kernels: 16.9 us -> 12.2 us
where the time goes in v3:
time: 239 us; the launch traced here: 238 us
  blocking collectives  184 us (77%)
  starting transfers between devices  35.3 us (15%)
  Pallas kernels  12.2 us (5%)
  other arithmetic  2.94 us (1%)
    all_to_all x7, blocking collectives, exchange(): return lax.all_to_all(x, axis, 0, 0, tiled=True)  130 us
    ppermute x3, starting transfers between devices, other_core(): return lax.ppermute(x, 'core', swap)  35.3 us
    all_gather x1, blocking collectives, backward(): full = lax.all_gather(fresh, 'z')  27.9 us
    all_gather x1, blocking collectives, first_backward(): full = lax.all_gather(piece, 'z')  26.2 us
    pallas_call x2, Pallas kernels, forward(): part, norms = apply(*slots, *turned, vec, full, first, second)  4.94 us
  transfers between devices with their start and end apart: 3, of which 2 were waited for; matrix products, arithmetic and copies ran while one was open for 0% of the time, Pallas kernels for 0%

profile of v3, /device:TPU:1, one launch (start us, length us, event | category | flops | bytes accessed | tf_op | source)
XLA Modules:
  0.0 238.5 jit_solution(14349344910866754865)
XLA Ops:
  0.0 0.7 select_bitcast_fusion
  0.7 0.7 fusion
  1.4 8.8 %collective-permute-start = (f32[40,128]{1,0:T(8,128)S(1)}, f32[40,128]{1,0:T(8,128)S(1)}, u32[]{:S(2)}, u32[]{:S(2)}) collective-permute-start(f32[40,128]{1,0:T(8,128)S(1)} %select_maximum_fusion), channel_id=1, source_target_pairs={{0,1},{1,0},{2,3},{3,2},{4,5},{5,4},{6,7},{7,6},{8,9},{9,8},{10,11... | collective-permute-start | bytes 61448 | tf_op jit(solution)/shard_map/ppermute | solution.py:281
  10.2 0.8 collective-permute-done
  11.1 2.2 collective-permute-start.1
  13.3 0.7 bitcast_select_fusion.1
  14.1 26.2 %all-gather = f32[1024,128]{1,0:T(8,128)S(1)} all-gather(f32[64,128]{1,0:T(8,128)S(1)} %pad_maximum_fusion.old), channel_id=2, replica_groups=mesh['row'=16,'z'=16,'core'=2] {'z'}, dimensions={0}, use_global_device_ids=true | all-gather | bytes 557056 | tf_op jit(solution)/shard_map/all_gather | solution.py:302
  40.3 2.2 copy-done
  42.5 4.3 %apply_first.1 = (f32[16,72,128]{2,1,0:T(8,128)S(1)}, bf16[64,128,128]{2,1,0:T(8,128)(2,1)S(1)}, bf16[64,128,128]{2,1,0:T(8,128)(2,1)S(1)}, bf16[64,128,128]{2,1...) custom-call(s32[3,64]{1,0:T(4,128)S(1)} %get-tuple-element.64.slots0, ...), custom_call_target="tpu_custom_call" | custom-call | tf_op jit(solution)/shard_map/apply_first/pallas_call | solution.py:307
  46.7 15.9 %all_to_all.37.got = f32[16,72,128]{2,1,0:T(8,128)S(1)} all-to-all(f32[16,72,128]{2,1,0:T(8,128)S(1)} %get-tuple-element.41), channel_id=1, replica_groups=mesh['row'=16,'z'=16,'core'=2] {'row'}, dimensions={0} | all-to-all | bytes 1179648 | tf_op jit(solution)/shard_map/all_to_all | solution.py:278
  62.6 0.2 first_cols.1
  62.8 11.9 %all_to_all.38.vec = f32[16,64,128]{2,1,0:T(8,128)S(1)} all-to-all(f32[16,64,128]{2,1,0:T(8,128)S(1)} %get-tuple-element.42), channel_id=1, replica_groups=mesh['row'=16,'z'=16,'core'=2] {'row'}, dimensions={0} | all-to-all | bytes 1048576 | tf_op jit(solution)/shard_map/all_to_all | solution.py:278
  74.7 2.5 %apply_plain.2 = (f32[16,64,128]{2,1,0:T(8,128)S(1)}, f32[8,128]{1,0:T(8,128)S(1)}) custom-call(s32[3,64]{1,0:T(4,128)S(1)} %get-tuple-element.64.slots0, s32[3,64]{1,0:T(4,128)S(1)} %slice_convert_fusion.slots1, bf16[64,128,128]{2,1,0:T(8,128)(2,1)S(1)} %get-tuple-element.37.hi0, bf16[64,128,128]{2,1,0:T(8,128)(2,1)S(1)} %get-tuple-element.38.lo0, ...), custom_call_target="tpu_custom_call" | custom-call | tf_op jit(solution)/shard_map/apply_plain/pallas_call | solution.py:321
  77.2 23.0 %all_to_all.39.got = f32[16,64,128]{2,1,0:T(8,128)S(1)} all-to-all(f32[16,64,128]{2,1,0:T(8,128)S(1)} %get-tuple-element.44), channel_id=1, replica_groups=mesh['row'=16,'z'=16,'core'=2] {'z'}, dimensions={0} | all-to-all | bytes 1048576 | tf_op jit(solution)/shard_map/all_to_all | solution.py:278
  100.2 27.9 %all-gather.1 = f32[1152,128]{1,0:T(8,128)S(1)} all-gather(f32[72,128]{1,0:T(8,128)S(1)} %rows.2.old), channel_id=3, replica_groups=mesh['row'=16,'z'=16,'core'=2] {'z'}, dimensions={0}, use_global_device_ids=true | all-gather | bytes 626688 | tf_op jit(solution)/shard_map/all_gather | solution.py:311
  128.1 2.4 apply_transposed.1
  130.5 12.3 %all_to_all.40.got = f32[16,72,128]{2,1,0:T(8,128)S(1)} all-to-all(f32[16,72,128]{2,1,0:T(8,128)S(1)} %get-tuple-element.47), channel_id=1, replica_groups=mesh['row'=16,'z'=16,'core'=2] {'row'}, dimensions={0} | all-to-all | bytes 1179648 | tf_op jit(solution)/shard_map/all_to_all | solution.py:278
  143.0 11.9 %all_to_all.41.vec = f32[16,64,128]{2,1,0:T(8,128)S(1)} all-to-all(f32[16,64,128]{2,1,0:T(8,128)S(1)} %get-tuple-element.51), channel_id=1, replica_groups=mesh['row'=16,'z'=16,'core'=2] {'row'}, dimensions={0} | all-to-all | bytes 1048576 | tf_op jit(solution)/shard_map/all_to_all | solution.py:278
  154.9 2.5 %apply_plain.3 = (f32[16,64,128]{2,1,0:T(8,128)S(1)}, f32[8,128]{1,0:T(8,128)S(1)}) custom-call(s32[3,64]{1,0:T(4,128)S(1)} %get-tuple-element.64.slots0, s32[3,64]{1,0:T(4,128)S(1)} %slice_convert_fusion.slots1, bf16[64,128,128]{2,1,0:T(8,128)(2,1)S(1)} %get-tuple-element.37.hi0, bf16[64,128,128]{2,1,0:T(8,128)(2,1)S(1)} %get-tuple-element.38.lo0, ...), custom_call_target="tpu_custom_call" | custom-call | tf_op jit(solution)/shard_map/apply_plain/pallas_call | solution.py:321
  157.4 25.4 %all_to_all.42.got = f32[16,64,128]{2,1,0:T(8,128)S(1)} all-to-all(f32[16,64,128]{2,1,0:T(8,128)S(1)} %get-tuple-element.54), channel_id=1, replica_groups=mesh['row'=16,'z'=16,'core'=2] {'z'}, dimensions={0} | all-to-all | bytes 1048576 | tf_op jit(solution)/shard_map/all_to_all | solution.py:278
  183.1 29.4 %all_to_all.43 = f32[256,1,128]{2,1,0:T(1,128)S(1)} all-to-all(f32[256,1,128]{2,1,0:T(1,128)S(1)} %broadcast_in_dim.19), channel_id=1, replica_groups=mesh['row'=16,'z'=16,'core'=2] {'row','z'}, dimensions={0} | all-to-all | bytes 262144 | tf_op jit(solution)/shard_map/all_to_all | solution.py:278
  212.8 24.3 %collective-permute-start.2 = (f32[32,128]{1,0:T(8,128)S(1)}, f32[32,128]{1,0:T(8,128)S(1)}, u32[]{:S(2)}, u32[]{:S(2)}) collective-permute-start(f32[32,128]{1,0:T(8,128)S(1)} %slice.33), channel_id=1, source_target_pairs={{0,1},{1,0},{2,3},{3,2},{4,5},{5,4},{6,7},{7,6},{8,9},{9,8},{10,11... | collective-permute-start | bytes 49160 | tf_op jit(solution)/shard_map/ppermute | solution.py:281
  237.0 0.8 collective-permute-done.2
  237.9 0.6 maximum_bitcast_fusion
  (16 shorter events, 0.7 us)
Async XLA Ops:
  1.4 9.6 %collective-permute-start = (f32[40,128]{1,0:T(8,128)S(1)}, f32[40,128]{1,0:T(8,128)S(1)}, u32[]{:S(2)}, u32[]{:S(2)}) collective-permute-start(f32[40,128]{1,0:T(8,128)S(1)} %select_maximum_fusion), channel_id=1, source_target_pairs={{0,1},{1,0},{2,3},{3,2},{4,5},{5,4},{6,7},{7,6},{8,9},{9,8},{10,11... | collective-permute-start | bytes 61448 | tf_op jit(solution)/shard_map/ppermute | solution.py:281
  11.1 29.2 %collective-permute-start.1 = (f32[64,128,128]{2,1,0:T(8,128)}, f32[64,128,128]{2,1,0:T(8,128)S(1)}, u32[]{:S(2)}, u32[]{:S(2)}) collective-permute-start(f32[64,128,128]{2,1,0:T(8,128)} %bitcast.20), channel_id=1, source_target_pairs={{0,1},{1,0},{2,3},{3,2},{4,5},{5,4},{6,7},{7,6},{8,9},{9,8},{10,11... | collective-permute-start | bytes 12582920 | tf_op jit(solution)/shard_map/ppermute | solution.py:281
  40.3 2.2 copy-start
  212.8 25.1 %collective-permute-start.2 = (f32[32,128]{1,0:T(8,128)S(1)}, f32[32,128]{1,0:T(8,128)S(1)}, u32[]{:S(2)}, u32[]{:S(2)}) collective-permute-start(f32[32,128]{1,0:T(8,128)S(1)} %slice.33), channel_id=1, source_target_pairs={{0,1},{1,0},{2,3},{3,2},{4,5},{5,4},{6,7},{7,6},{8,9},{9,8},{10,11... | collective-permute-start | bytes 49160 | tf_op jit(solution)/shard_map/ppermute | solution.py:281

commit v4 on v3

--- a/solution.py
+++ b/solution.py
@@ -7,7 +7,6 @@
 
 W = 128
 SLOTS = 64
-GROUP = 16
 HALF = 32
 RBL = 32
 CBL = 16
@@ -25,7 +24,6 @@
 
 SMEM = pl.BlockSpec(memory_space=pltpu.SMEM)
 VMEM = pl.BlockSpec(memory_space=pltpu.VMEM)
-HBM = pl.BlockSpec(memory_space=pltpu.HBM)
 PARAMS = pltpu.CompilerParams(vmem_limit_bytes=16 << 20)
 
 
@@ -101,30 +99,34 @@
         out[c, 2 * HALF :] = norms
 
 
-def first_backward_kernel(slots0, slots1, mats0, mats1, vec, out, *rest):
-    kept, (blocks, arrived, parts, acc) = rest[:8], rest[8:]
-    copies = []
-    for index in range(SLOTS // GROUP):
-        some = pl.ds(index * GROUP, GROUP)
-        copies.append(pltpu.make_async_copy(mats0.at[some], blocks.at[some], arrived.at[index]))
-        copies[index].start()
+def first_products(slots, mats, kept, parts, acc):
+    hi, lo, hi_t, lo_t = kept
+    acc[...] = jnp.zeros_like(acc)
+    for s in range(SLOTS):
+        block = mats[s]
+        high, low = halves(block)
+        hi[s], lo[s] = high, low
+        hi_t[s], lo_t[s] = halves(block.T)
+        add_product(slots, s, 0, high, low, parts, acc, by_row, by_col, CBL)
+
+
+def first_other_kernel(slots, mats, vec, hi, lo, hi_t, lo_t, parts, part, norms, acc):
     squares = jnp.zeros((2 * HALF, W), F32)
     for z in range(NZ):
         x = vec[z]
         squares += x * x
         store_tiles(parts, 2 * z, 2 * z + 1, x)
-    acc[...] = jnp.zeros_like(acc)
-    for side, slots, mats in ((1, slots1, mats1), (0, slots0, blocks)):
-        hi, lo, hi_t, lo_t = kept[4 * side : 4 * side + 4]
-        for s in range(SLOTS):
-            if side == 0 and s % GROUP == 0:
-                copies[s // GROUP].wait()
-            block = mats[s]
-            high, low = halves(block)
-            hi[s], lo[s] = high, low
-            hi_t[s], lo_t[s] = halves(block.T)
-            add_product(slots, s, side, high, low, parts, acc, by_row, by_col, 2 * CBL)
-    emit_cols(out, acc, squares)
+    norms[...] = norm_rows(squares)
+    first_products(slots, mats, (hi, lo, hi_t, lo_t), parts, acc)
+    part[...] = acc[:CBL]
+
+
+def first_own_kernel(slots, mats, parts, part, norms, hi, lo, hi_t, lo_t, out, acc):
+    first_products(slots, mats, (hi, lo, hi_t, lo_t), parts, acc)
+    for c in range(CBL):
+        out[c, :HALF] = acc[c]
+        out[c, HALF : 2 * HALF] = part[c]
+        out[c, 2 * HALF :] = norms[...]
 
 
 def backward_kernel(slots0, slots1, hi0, lo0, hi1, lo1, vec, out, scale, factor, parts, acc):
@@ -235,7 +237,7 @@
     scale[...] = spread(root(col_at(got[...], 0)))
 
 
-def call(kernel, name, specs, outs, scratch=()):
+def call(kernel, name, specs, outs, scratch=(), cost=None):
     return pl.pallas_call(
         kernel,
         out_shape=outs,
@@ -243,6 +245,7 @@
         out_specs=jax.tree.map(lambda _: VMEM, outs),
         scratch_shapes=scratch,
         compiler_params=PARAMS,
+        cost_estimate=cost,
         name=name,
     )
 
@@ -300,12 +303,16 @@
 
     def first_backward():
         full = lax.all_gather(piece, "z")
-        outs = (wide,) + (halved,) * 8
-        held = (pltpu.VMEM((SLOTS, W, W), F32), pltpu.SemaphoreType.DMA((SLOTS // GROUP,)))
-        in_specs = [SMEM] * 2 + [HBM] + [VMEM] * 2
-        apply = call(first_backward_kernel, "apply_first", in_specs, outs, held + scratch(RBL, 2 * CBL))
-        part, hi0, lo0, hi_t0, lo_t0, hi1, lo1, hi_t1, lo_t1 = apply(*slots, mats, other_mats, full)
-        return exchange(part, "row"), full, (hi0, lo0, hi1, lo1), (hi_t0, lo_t0, hi_t1, lo_t1)
+        parts = jax.ShapeDtypeStruct((RBL, 2 * HALF, W), BF16)
+        acc = (pltpu.VMEM((CBL + 1, HALF, W), F32),)
+        outs = (halved,) * 4 + (parts, array(CBL, HALF, W), rows_tile)
+        cost = pl.CostEstimate(flops=SLOTS * 2**22, bytes_accessed=SLOTS * 3 * 2**16, transcendentals=0)
+        apply = call(first_other_kernel, "apply_first_other", [SMEM] + [VMEM] * 2, outs, acc, cost)
+        *kept1, parts, part, norms = apply(slots[1], other_mats, full)
+        outs = (halved,) * 4 + (wide,)
+        apply = call(first_own_kernel, "apply_first_own", [SMEM] + [VMEM] * 4, outs, acc, cost)
+        *kept0, out = apply(slots[0], mats, parts, part, norms)
+        return exchange(out, "row"), full, (*kept0[:2], *kept1[:2]), (*kept0[2:], *kept1[2:])
 
     def backward(fresh):
         full = lax.all_gather(fresh, "z")

time: 239 us -> 237 us (level)
  no operation moved by 1% of the time
where the time goes in v4:
time: 237 us; the launch traced here: 236 us
  blocking collectives  184 us (78%)
  starting transfers between devices  35.2 us (15%)
  Pallas kernels  12.4 us (5%)
  other arithmetic  2.94 us (1%)
    all_to_all x7, blocking collectives, exchange(): return lax.all_to_all(x, axis, 0, 0, tiled=True)  130 us
    ppermute x3, starting transfers between devices, other_core(): return lax.ppermute(x, 'core', swap)  35.2 us
    all_gather x1, blocking collectives, backward(): full = lax.all_gather(fresh, 'z')  27.9 us
    all_gather x1, blocking collectives, first_backward(): full = lax.all_gather(piece, 'z')  26.2 us
    pallas_call x2, Pallas kernels, forward(): part, norms = apply(*slots, *turned, vec, full, first, second)  5 us
  transfers between devices with their start and end apart: 3, of which 2 were waited for; matrix products, arithmetic and copies ran while one was open for 0% of the time, Pallas kernels for 0%

profile of v4, /device:TPU:1, one launch (start us, length us, event | category | flops | bytes accessed | tf_op | source)
XLA Modules:
  0.0 236.1 jit_solution(8174424543584948747)
XLA Ops:
  0.0 0.7 select_bitcast_fusion
  0.7 0.7 fusion
  1.4 8.8 %collective-permute-start = (f32[40,128]{1,0:T(8,128)S(1)}, f32[40,128]{1,0:T(8,128)S(1)}, u32[]{:S(2)}, u32[]{:S(2)}) collective-permute-start(f32[40,128]{1,0:T(8,128)S(1)} %select_maximum_fusion), channel_id=1, source_target_pairs={{0,1},{1,0},{2,3},{3,2},{4,5},{5,4},{6,7},{7,6},{8,9},{9,8},{10,11... | collective-permute-start | bytes 61448 | tf_op jit(solution)/shard_map/ppermute | solution.py:284
  10.2 0.8 collective-permute-done
  11.1 2.2 collective-permute-start.1
  13.3 0.7 bitcast_select_fusion.1
  14.1 26.2 %all-gather = f32[1024,128]{1,0:T(8,128)S(1)} all-gather(f32[64,128]{1,0:T(8,128)S(1)} %pad_maximum_fusion.old), channel_id=2, replica_groups=mesh['row'=16,'z'=16,'core'=2] {'z'}, dimensions={0}, use_global_device_ids=true | all-gather | bytes 557056 | tf_op jit(solution)/shard_map/all_gather | solution.py:305
  40.3 2.3 apply_first_other.1
  42.6 2.1 apply_first_own.1
  44.7 15.9 %all_to_all.37.got = f32[16,72,128]{2,1,0:T(8,128)S(1)} all-to-all(f32[16,72,128]{2,1,0:T(8,128)S(1)} %get-tuple-element.47), channel_id=1, replica_groups=mesh['row'=16,'z'=16,'core'=2] {'row'}, dimensions={0} | all-to-all | bytes 1179648 | tf_op jit(solution)/shard_map/all_to_all | solution.py:281
  60.6 0.2 first_cols.1
  60.7 11.9 %all_to_all.38.vec = f32[16,64,128]{2,1,0:T(8,128)S(1)} all-to-all(f32[16,64,128]{2,1,0:T(8,128)S(1)} %get-tuple-element.48), channel_id=1, replica_groups=mesh['row'=16,'z'=16,'core'=2] {'row'}, dimensions={0} | all-to-all | bytes 1048576 | tf_op jit(solution)/shard_map/all_to_all | solution.py:281
  72.6 2.5 %apply_plain.2 = (f32[16,64,128]{2,1,0:T(8,128)S(1)}, f32[8,128]{1,0:T(8,128)S(1)}) custom-call(s32[3,64]{1,0:T(4,128)S(1)} %get-tuple-element.70.slots.slots0, s32[3,64]{1,0:T(4,128)S(1)} %slice_convert_fusion.slots.slots1, bf16[64,128,128]{2,1,0:T(8,128)(2,1)S(1)} %get-tuple-element.43.hi0, bf16[64,128,128]{2,1,0:T(8,128)(2,1)S(1)} %get-tuple-element.44.lo0, ...), custom_call_target="tpu_custom_call" | custom-call | tf_op jit(solution)/shard_map/apply_plain/pallas_call | solution.py:328
  75.1 22.9 %all_to_all.39.got = f32[16,64,128]{2,1,0:T(8,128)S(1)} all-to-all(f32[16,64,128]{2,1,0:T(8,128)S(1)} %get-tuple-element.50), channel_id=1, replica_groups=mesh['row'=16,'z'=16,'core'=2] {'z'}, dimensions={0} | all-to-all | bytes 1048576 | tf_op jit(solution)/shard_map/all_to_all | solution.py:281
  98.0 27.9 %all-gather.1 = f32[1152,128]{1,0:T(8,128)S(1)} all-gather(f32[72,128]{1,0:T(8,128)S(1)} %rows.2.old), channel_id=3, replica_groups=mesh['row'=16,'z'=16,'core'=2] {'z'}, dimensions={0}, use_global_device_ids=true | all-gather | bytes 626688 | tf_op jit(solution)/shard_map/all_gather | solution.py:318
  125.9 2.4 %apply_transposed.1 = (f32[16,72,128]{2,1,0:T(8,128)S(1)}, f32[64,128]{1,0:T(8,128)S(1)}, f32[64,128]{1,0:T(8,128)S(1)}) custom-call(s32[3,64]{1,0:T(4,128)S(1)} %get-tuple-element.70.slots.slots0, s32[3,64]{1,0:T(4,128)S(1)} %slice_convert_fusion.slots.slots1, bf16[64,128,128]{2,1,0:T(8,128)(2,1)S(1)} %get-tuple-element.39.hi0, ...), custom_call_target="tpu_custom_call" | custom-call | tf_op jit(solution)/shard_map/apply_transposed/pallas_call | solution.py:320
  128.3 12.4 %all_to_all.40.got = f32[16,72,128]{2,1,0:T(8,128)S(1)} all-to-all(f32[16,72,128]{2,1,0:T(8,128)S(1)} %get-tuple-element.53), channel_id=1, replica_groups=mesh['row'=16,'z'=16,'core'=2] {'row'}, dimensions={0} | all-to-all | bytes 1179648 | tf_op jit(solution)/shard_map/all_to_all | solution.py:281
  140.8 11.9 %all_to_all.41.vec = f32[16,64,128]{2,1,0:T(8,128)S(1)} all-to-all(f32[16,64,128]{2,1,0:T(8,128)S(1)} %get-tuple-element.57), channel_id=1, replica_groups=mesh['row'=16,'z'=16,'core'=2] {'row'}, dimensions={0} | all-to-all | bytes 1048576 | tf_op jit(solution)/shard_map/all_to_all | solution.py:281
  152.7 2.5 %apply_plain.3 = (f32[16,64,128]{2,1,0:T(8,128)S(1)}, f32[8,128]{1,0:T(8,128)S(1)}) custom-call(s32[3,64]{1,0:T(4,128)S(1)} %get-tuple-element.70.slots.slots0, s32[3,64]{1,0:T(4,128)S(1)} %slice_convert_fusion.slots.slots1, bf16[64,128,128]{2,1,0:T(8,128)(2,1)S(1)} %get-tuple-element.43.hi0, bf16[64,128,128]{2,1,0:T(8,128)(2,1)S(1)} %get-tuple-element.44.lo0, ...), custom_call_target="tpu_custom_call" | custom-call | tf_op jit(solution)/shard_map/apply_plain/pallas_call | solution.py:328
  155.2 25.3 %all_to_all.42.got = f32[16,64,128]{2,1,0:T(8,128)S(1)} all-to-all(f32[16,64,128]{2,1,0:T(8,128)S(1)} %get-tuple-element.60), channel_id=1, replica_groups=mesh['row'=16,'z'=16,'core'=2] {'z'}, dimensions={0} | all-to-all | bytes 1048576 | tf_op jit(solution)/shard_map/all_to_all | solution.py:281
  180.8 29.5 %all_to_all.43 = f32[256,1,128]{2,1,0:T(1,128)S(1)} all-to-all(f32[256,1,128]{2,1,0:T(1,128)S(1)} %broadcast_in_dim.19), channel_id=1, replica_groups=mesh['row'=16,'z'=16,'core'=2] {'row','z'}, dimensions={0} | all-to-all | bytes 262144 | tf_op jit(solution)/shard_map/all_to_all | solution.py:281
  210.5 24.1 %collective-permute-start.2 = (f32[32,128]{1,0:T(8,128)S(1)}, f32[32,128]{1,0:T(8,128)S(1)}, u32[]{:S(2)}, u32[]{:S(2)}) collective-permute-start(f32[32,128]{1,0:T(8,128)S(1)} %slice.33), channel_id=1, source_target_pairs={{0,1},{1,0},{2,3},{3,2},{4,5},{5,4},{6,7},{7,6},{8,9},{9,8},{10,11... | collective-permute-start | bytes 49160 | tf_op jit(solution)/shard_map/ppermute | solution.py:284
  234.7 0.8 collective-permute-done.2
  235.5 0.6 maximum_bitcast_fusion
  (17 shorter events, 0.7 us)
Async XLA Ops:
  1.4 9.6 %collective-permute-start = (f32[40,128]{1,0:T(8,128)S(1)}, f32[40,128]{1,0:T(8,128)S(1)}, u32[]{:S(2)}, u32[]{:S(2)}) collective-permute-start(f32[40,128]{1,0:T(8,128)S(1)} %select_maximum_fusion), channel_id=1, source_target_pairs={{0,1},{1,0},{2,3},{3,2},{4,5},{5,4},{6,7},{7,6},{8,9},{9,8},{10,11... | collective-permute-start | bytes 61448 | tf_op jit(solution)/shard_map/ppermute | solution.py:284
  11.1 29.2 %collective-permute-start.1 = (f32[64,128,128]{2,1,0:T(8,128)}, f32[64,128,128]{2,1,0:T(8,128)S(1)}, u32[]{:S(2)}, u32[]{:S(2)}) collective-permute-start(f32[64,128,128]{2,1,0:T(8,128)} %bitcast.20), channel_id=1, source_target_pairs={{0,1},{1,0},{2,3},{3,2},{4,5},{5,4},{6,7},{7,6},{8,9},{9,8},{10,11... | collective-permute-start | bytes 12582920 | tf_op jit(solution)/shard_map/ppermute | solution.py:284
  40.3 2.3 copy-start
  210.5 25.0 %collective-permute-start.2 = (f32[32,128]{1,0:T(8,128)S(1)}, f32[32,128]{1,0:T(8,128)S(1)}, u32[]{:S(2)}, u32[]{:S(2)}) collective-permute-start(f32[32,128]{1,0:T(8,128)S(1)} %slice.33), channel_id=1, source_target_pairs={{0,1},{1,0},{2,3},{3,2},{4,5},{5,4},{6,7},{7,6},{8,9},{9,8},{10,11... | collective-permute-start | bytes 49160 | tf_op jit(solution)/shard_map/ppermute | solution.py:284

commit v5 on v4

--- a/solution.py
+++ b/solution.py
@@ -108,6 +108,16 @@
         hi[s], lo[s] = high, low
         hi_t[s], lo_t[s] = halves(block.T)
         add_product(slots, s, 0, high, low, parts, acc, by_row, by_col, CBL)
+
+
+def pack_kernel(core, data, rows, cols, valid, mine, slots, message):
+    me = core[0]
+    mine[...] = data[pl.ds(pl.multiple_of(me * HALF, HALF), HALF)]
+    message[:HALF] = data[pl.ds(pl.multiple_of((1 - me) * HALF, HALF), HALF)]
+    message[HALF:] = jnp.zeros((PAD, W), F32)
+    for index, values in enumerate((rows, cols, valid)):
+        slots[index : index + 1] = values[...]
+        message[HALF + index : HALF + index + 1, :SLOTS] = values[...].astype(F32)
 
 
 def first_other_kernel(slots, mats, vec, hi, lo, hi_t, lo_t, parts, part, norms, acc):
@@ -289,12 +299,11 @@
     def scratch(sources, targets):
         return (pltpu.VMEM((sources, 2 * HALF, W), BF16), pltpu.VMEM((targets + 1, HALF, W), F32))
 
-    pieces = rhs[0, 0].reshape(2, HALF, W)
-    mine = jnp.where(me == 0, pieces[0], pieces[1])
-    rest = jnp.where(me == 0, pieces[1], pieces[0])
-    own_slots = jnp.stack([block_rows[0, 0], block_cols[0, 0], block_valid[0, 0]])
-    listed = jnp.pad(own_slots.astype(F32), ((0, PAD - 3), (0, W - SLOTS)))
-    got = other_core(jnp.concatenate([rest, listed]))
+    outs = (array(HALF, W), jax.ShapeDtypeStruct((3, SLOTS), jnp.int32), array(HALF + PAD, W))
+    lists = (block_rows[0], block_cols[0], block_valid[0])
+    pack = call(pack_kernel, "pack", [SMEM] + [VMEM] * 4, outs)
+    mine, own_slots, message = pack(me.astype(jnp.int32).reshape(1), rhs[0, 0], *lists)
+    got = other_core(message)
     slots = (own_slots, got[HALF : HALF + 3, :SLOTS].astype(jnp.int32))
     piece = in_order(mine, got[:HALF])
     other_mats, _ = lax.optimization_barrier((mats, got))

time: 237 us -> 239 us (level)
  local copies, waits for them, and re-layouts: 0.08 us -> 2.8 us
    unnamed x2 -> x10, local copies, waits for them, and re-layouts: 0.01 us -> 2.73 us
where the time goes in v5:
time: 239 us
  blocking collectives  184 us (77%)
  starting transfers between devices  35.2 us (15%)
  Pallas kernels  14.3 us (6%)
  local copies, waits for them, and re-layouts  2.8 us (1%)
    all_to_all x7, blocking collectives, exchange(): return lax.all_to_all(x, axis, 0, 0, tiled=True)  130 us
    ppermute x3, starting transfers between devices, other_core(): return lax.ppermute(x, 'core', swap)  35.2 us
    all_gather x1, blocking collectives, backward(): full = lax.all_gather(fresh, 'z')  27.9 us
    all_gather x1, blocking collectives, first_backward(): full = lax.all_gather(piece, 'z')  26.2 us
    pallas_call x2, Pallas kernels, forward(): part, norms = apply(*slots, *turned, vec, full, first, second)  5.25 us
  transfers between devices with their start and end apart: 3, of which 2 were waited for; matrix products, arithmetic and copies ran while one was open for 0% of the time, Pallas kernels for 0%

profile of v5, /device:TPU:1, one launch (start us, length us, event | category | flops | bytes accessed | tf_op | source)
XLA Modules:
  0.0 238.6 jit_solution(17367656613910288529)
XLA Ops:
  0.0 0.8 copy-done.1
  0.8 0.7 copy-done.2
  1.4 0.7 copy-done.3
  2.1 0.7 copy-done.4
  2.7 8.8 %collective-permute-start = (f32[40,128]{1,0:T(8,128)S(1)}, f32[40,128]{1,0:T(8,128)S(1)}, u32[]{:S(2)}, u32[]{:S(2)}) collective-permute-start(f32[40,128]{1,0:T(8,128)S(1)} %get-tuple-element.39), channel_id=1, source_target_pairs={{0,1},{1,0},{2,3},{3,2},{4,5},{5,4},{6,7},{7,6},{8,9},{9,8},{10,11... | collective-permute-start | bytes 61448 | tf_op jit(solution)/shard_map/ppermute | solution.py:294
  11.5 0.8 collective-permute-done
  12.3 2.2 collective-permute-start.1
  14.6 26.2 %all-gather = f32[1024,128]{1,0:T(8,128)S(1)} all-gather(f32[64,128]{1,0:T(8,128)S(1)} %pad_maximum_fusion.old), channel_id=2, replica_groups=mesh['row'=16,'z'=16,'core'=2] {'z'}, dimensions={0}, use_global_device_ids=true | all-gather | bytes 557056 | tf_op jit(solution)/shard_map/all_gather | solution.py:314
  40.8 4.0 %apply_first_other.1 = (bf16[64,128,128]{2,1,0:T(8,128)(2,1)S(1)}, bf16[64,128,128]{2,1,0:T(8,128)(2,1)S(1)}, bf16[64,128,128]{2,1,0:T(8,128)(2,1)S(1)}, bf16[64...) custom-call(s32[3,64]{1,0:T(4,128)S(1)} %slice_convert_fusion.slots., ...), custom_call_target="tpu_custom_call" | custom-call | flops 268435456 | bytes 12582912 | tf_op jit(solution)/shard_map/apply_first_other/pallas_call | solution.py:320
  44.9 2.1 apply_first_own.1
  46.9 15.9 %all_to_all.37.got = f32[16,72,128]{2,1,0:T(8,128)S(1)} all-to-all(f32[16,72,128]{2,1,0:T(8,128)S(1)} %get-tuple-element.53), channel_id=1, replica_groups=mesh['row'=16,'z'=16,'core'=2] {'row'}, dimensions={0} | all-to-all | bytes 1179648 | tf_op jit(solution)/shard_map/all_to_all | solution.py:291
  63.0 11.9 %all_to_all.38.vec = f32[16,64,128]{2,1,0:T(8,128)S(1)} all-to-all(f32[16,64,128]{2,1,0:T(8,128)S(1)} %get-tuple-element.54), channel_id=1, replica_groups=mesh['row'=16,'z'=16,'core'=2] {'row'}, dimensions={0} | all-to-all | bytes 1048576 | tf_op jit(solution)/shard_map/all_to_all | solution.py:291
  74.9 2.6 %apply_plain.2 = (f32[16,64,128]{2,1,0:T(8,128)S(1)}, f32[8,128]{1,0:T(8,128)S(1)}) custom-call(s32[3,64]{1,0:T(4,128)S(1)} %get-tuple-element.38.slots.slots0, s32[3,64]{1,0:T(4,128)S(1)} %slice_convert_fusion.slots.slots1, bf16[64,128,128]{2,1,0:T(8,128)(2,1)S(1)} %get-tuple-element.49.hi0, bf16[64,128,128]{2,1,0:T(8,128)(2,1)S(1)} %get-tuple-element.50.lo0, ...), custom_call_target="tpu_custom_call" | custom-call | tf_op jit(solution)/shard_map/apply_plain/pallas_call | solution.py:337
  77.5 22.9 %all_to_all.39.got = f32[16,64,128]{2,1,0:T(8,128)S(1)} all-to-all(f32[16,64,128]{2,1,0:T(8,128)S(1)} %get-tuple-element.56), channel_id=1, replica_groups=mesh['row'=16,'z'=16,'core'=2] {'z'}, dimensions={0} | all-to-all | bytes 1048576 | tf_op jit(solution)/shard_map/all_to_all | solution.py:291
  100.4 27.9 %all-gather.1 = f32[1152,128]{1,0:T(8,128)S(1)} all-gather(f32[72,128]{1,0:T(8,128)S(1)} %rows.2.old), channel_id=3, replica_groups=mesh['row'=16,'z'=16,'core'=2] {'z'}, dimensions={0}, use_global_device_ids=true | all-gather | bytes 626688 | tf_op jit(solution)/shard_map/all_gather | solution.py:327
  128.3 2.3 apply_transposed.1
  130.7 12.4 %all_to_all.40.got = f32[16,72,128]{2,1,0:T(8,128)S(1)} all-to-all(f32[16,72,128]{2,1,0:T(8,128)S(1)} %get-tuple-element.59), channel_id=1, replica_groups=mesh['row'=16,'z'=16,'core'=2] {'row'}, dimensions={0} | all-to-all | bytes 1179648 | tf_op jit(solution)/shard_map/all_to_all | solution.py:291
  143.3 11.9 %all_to_all.41.vec = f32[16,64,128]{2,1,0:T(8,128)S(1)} all-to-all(f32[16,64,128]{2,1,0:T(8,128)S(1)} %get-tuple-element.63), channel_id=1, replica_groups=mesh['row'=16,'z'=16,'core'=2] {'row'}, dimensions={0} | all-to-all | bytes 1048576 | tf_op jit(solution)/shard_map/all_to_all | solution.py:291
  155.2 2.6 %apply_plain.3 = (f32[16,64,128]{2,1,0:T(8,128)S(1)}, f32[8,128]{1,0:T(8,128)S(1)}) custom-call(s32[3,64]{1,0:T(4,128)S(1)} %get-tuple-element.38.slots.slots0, s32[3,64]{1,0:T(4,128)S(1)} %slice_convert_fusion.slots.slots1, bf16[64,128,128]{2,1,0:T(8,128)(2,1)S(1)} %get-tuple-element.49.hi0, bf16[64,128,128]{2,1,0:T(8,128)(2,1)S(1)} %get-tuple-element.50.lo0, ...), custom_call_target="tpu_custom_call" | custom-call | tf_op jit(solution)/shard_map/apply_plain/pallas_call | solution.py:337
  157.8 25.4 %all_to_all.42.got = f32[16,64,128]{2,1,0:T(8,128)S(1)} all-to-all(f32[16,64,128]{2,1,0:T(8,128)S(1)} %get-tuple-element.66), channel_id=1, replica_groups=mesh['row'=16,'z'=16,'core'=2] {'z'}, dimensions={0} | all-to-all | bytes 1048576 | tf_op jit(solution)/shard_map/all_to_all | solution.py:291
  183.4 29.3 %all_to_all.43 = f32[256,1,128]{2,1,0:T(1,128)S(1)} all-to-all(f32[256,1,128]{2,1,0:T(1,128)S(1)} %broadcast_in_dim.19), channel_id=1, replica_groups=mesh['row'=16,'z'=16,'core'=2] {'row','z'}, dimensions={0} | all-to-all | bytes 262144 | tf_op jit(solution)/shard_map/all_to_all | solution.py:291
  213.0 24.1 %collective-permute-start.2 = (f32[32,128]{1,0:T(8,128)S(1)}, f32[32,128]{1,0:T(8,128)S(1)}, u32[]{:S(2)}, u32[]{:S(2)}) collective-permute-start(f32[32,128]{1,0:T(8,128)S(1)} %slice.21), channel_id=1, source_target_pairs={{0,1},{1,0},{2,3},{3,2},{4,5},{5,4},{6,7},{7,6},{8,9},{9,8},{10,11... | collective-permute-start | bytes 49160 | tf_op jit(solution)/shard_map/ppermute | solution.py:294
  237.1 0.8 collective-permute-done.2
  238.0 0.6 maximum_bitcast_fusion
  (23 shorter events, 0.9 us)
Async XLA Ops:
  0.0 0.8 copy-start.1
  0.8 0.7 copy-start.2
  1.4 0.7 copy-start.3
  2.1 0.7 copy-start.4
  2.7 9.6 %collective-permute-start = (f32[40,128]{1,0:T(8,128)S(1)}, f32[40,128]{1,0:T(8,128)S(1)}, u32[]{:S(2)}, u32[]{:S(2)}) collective-permute-start(f32[40,128]{1,0:T(8,128)S(1)} %get-tuple-element.39), channel_id=1, source_target_pairs={{0,1},{1,0},{2,3},{3,2},{4,5},{5,4},{6,7},{7,6},{8,9},{9,8},{10,11... | collective-permute-start | bytes 61448 | tf_op jit(solution)/shard_map/ppermute | solution.py:294
  12.3 28.5 %collective-permute-start.1 = (f32[64,128,128]{2,1,0:T(8,128)}, f32[64,128,128]{2,1,0:T(8,128)}, u32[]{:S(2)}, u32[]{:S(2)}) collective-permute-start(f32[64,128,128]{2,1,0:T(8,128)} %bitcast.17), channel_id=1, source_target_pairs={{0,1},{1,0},{2,3},{3,2},{4,5},{5,4},{6,7},{7,6},{8,9},{9,8},{10,11... | collective-permute-start | bytes 12582920 | tf_op jit(solution)/shard_map/ppermute | solution.py:294
  40.8 4.0 %copy-start = (f32[1,1,64,128,128]{4,3,2,1,0:T(8,128)S(1)}, f32[1,1,64,128,128]{4,3,2,1,0:T(8,128)}, u32[]{:S(2)}) copy-start(f32[1,1,64,128,128]{4,3,2,1,0:T(8,128)} %param.5) | copy-start | bytes 12582916
  213.0 25.0 %collective-permute-start.2 = (f32[32,128]{1,0:T(8,128)S(1)}, f32[32,128]{1,0:T(8,128)S(1)}, u32[]{:S(2)}, u32[]{:S(2)}) collective-permute-start(f32[32,128]{1,0:T(8,128)S(1)} %slice.21), channel_id=1, source_target_pairs={{0,1},{1,0},{2,3},{3,2},{4,5},{5,4},{6,7},{7,6},{8,9},{9,8},{10,11... | collective-permute-start | bytes 49160 | tf_op jit(solution)/shard_map/ppermute | solution.py:294

commit v6 on v4

--- a/solution.py
+++ b/solution.py
@@ -292,6 +292,7 @@
     pieces = rhs[0, 0].reshape(2, HALF, W)
     mine = jnp.where(me == 0, pieces[0], pieces[1])
     rest = jnp.where(me == 0, pieces[1], pieces[0])
+    mine, rest = lax.optimization_barrier((mine, rest))
     own_slots = jnp.stack([block_rows[0, 0], block_cols[0, 0], block_valid[0, 0]])
     listed = jnp.pad(own_slots.astype(F32), ((0, PAD - 3), (0, W - SLOTS)))
     got = other_core(jnp.concatenate([rest, listed]))

time: 237 us -> 236 us (level)
  no operation moved by 1% of the time
where the time goes in v6:
time: 236 us
  blocking collectives  184 us (78%)
  starting transfers between devices  35.2 us (15%)
  Pallas kernels  12.6 us (5%)
    all_to_all x7, blocking collectives, exchange(): return lax.all_to_all(x, axis, 0, 0, tiled=True)  130 us
    ppermute x3, starting transfers between devices, other_core(): return lax.ppermute(x, 'core', swap)  35.2 us
    all_gather x1, blocking collectives, backward(): full = lax.all_gather(fresh, 'z')  27.9 us
    all_gather x1, blocking collectives, first_backward(): full = lax.all_gather(piece, 'z')  26.2 us
    pallas_call x2, Pallas kernels, forward(): part, norms = apply(*slots, *turned, vec, full, first, second)  5.18 us
  transfers between devices with their start and end apart: 3, of which 2 were waited for; matrix products, arithmetic and copies ran while one was open for 0% of the time, Pallas kernels for 0%

profile of v6, /device:TPU:1, one launch (start us, length us, event | category | flops | bytes accessed | tf_op | source)
XLA Modules:
  0.0 235.7 jit_solution(11801175519863838959)
XLA Ops:
  0.0 0.7 select_bitcast_fusion
  0.7 0.7 fusion
  1.4 8.8 %collective-permute-start = (f32[40,128]{1,0:T(8,128)S(1)}, f32[40,128]{1,0:T(8,128)S(1)}, u32[]{:S(2)}, u32[]{:S(2)}) collective-permute-start(f32[40,128]{1,0:T(8,128)S(1)} %select_maximum_fusion), channel_id=1, source_target_pairs={{0,1},{1,0},{2,3},{3,2},{4,5},{5,4},{6,7},{7,6},{8,9},{9,8},{10,11... | collective-permute-start | bytes 61448 | tf_op jit(solution)/shard_map/ppermute | solution.py:284
  10.2 0.8 collective-permute-done
  11.1 2.2 collective-permute-start.1
  13.4 26.2 %all-gather = f32[1024,128]{1,0:T(8,128)S(1)} all-gather(f32[64,128]{1,0:T(8,128)S(1)} %pad_maximum_fusion.old), channel_id=2, replica_groups=mesh['row'=16,'z'=16,'core'=2] {'z'}, dimensions={0}, use_global_device_ids=true | all-gather | bytes 557056 | tf_op jit(solution)/shard_map/all_gather | solution.py:306
  39.6 2.3 apply_first_other.1
  41.9 2.1 apply_first_own.1
  43.9 15.9 %all_to_all.37.got = f32[16,72,128]{2,1,0:T(8,128)S(1)} all-to-all(f32[16,72,128]{2,1,0:T(8,128)S(1)} %get-tuple-element.51), channel_id=1, replica_groups=mesh['row'=16,'z'=16,'core'=2] {'row'}, dimensions={0} | all-to-all | bytes 1179648 | tf_op jit(solution)/shard_map/all_to_all | solution.py:281
  59.8 0.2 first_cols.1
  60.0 11.9 %all_to_all.38.vec = f32[16,64,128]{2,1,0:T(8,128)S(1)} all-to-all(f32[16,64,128]{2,1,0:T(8,128)S(1)} %get-tuple-element.52), channel_id=1, replica_groups=mesh['row'=16,'z'=16,'core'=2] {'row'}, dimensions={0} | all-to-all | bytes 1048576 | tf_op jit(solution)/shard_map/all_to_all | solution.py:281
  71.9 2.6 %apply_plain.2 = (f32[16,64,128]{2,1,0:T(8,128)S(1)}, f32[8,128]{1,0:T(8,128)S(1)}) custom-call(s32[3,64]{1,0:T(4,128)S(1)} %get-tuple-element.76.slots.slots0, s32[3,64]{1,0:T(4,128)S(1)} %slice_convert_fusion.slots.slots1, bf16[64,128,128]{2,1,0:T(8,128)(2,1)S(1)} %get-tuple-element.47.hi0, bf16[64,128,128]{2,1,0:T(8,128)(2,1)S(1)} %get-tuple-element.48.lo0, ...), custom_call_target="tpu_custom_call" | custom-call | tf_op jit(solution)/shard_map/apply_plain/pallas_call | solution.py:329
  74.5 23.0 %all_to_all.39.got = f32[16,64,128]{2,1,0:T(8,128)S(1)} all-to-all(f32[16,64,128]{2,1,0:T(8,128)S(1)} %get-tuple-element.54), channel_id=1, replica_groups=mesh['row'=16,'z'=16,'core'=2] {'z'}, dimensions={0} | all-to-all | bytes 1048576 | tf_op jit(solution)/shard_map/all_to_all | solution.py:281
  97.5 27.9 %all-gather.1 = f32[1152,128]{1,0:T(8,128)S(1)} all-gather(f32[72,128]{1,0:T(8,128)S(1)} %rows.2.old), channel_id=3, replica_groups=mesh['row'=16,'z'=16,'core'=2] {'z'}, dimensions={0}, use_global_device_ids=true | all-gather | bytes 626688 | tf_op jit(solution)/shard_map/all_gather | solution.py:319
  125.4 2.4 %apply_transposed.1 = (f32[16,72,128]{2,1,0:T(8,128)S(1)}, f32[64,128]{1,0:T(8,128)S(1)}, f32[64,128]{1,0:T(8,128)S(1)}) custom-call(s32[3,64]{1,0:T(4,128)S(1)} %get-tuple-element.76.slots.slots0, s32[3,64]{1,0:T(4,128)S(1)} %slice_convert_fusion.slots.slots1, bf16[64,128,128]{2,1,0:T(8,128)(2,1)S(1)} %get-tuple-element.43.hi0, ...), custom_call_target="tpu_custom_call" | custom-call | tf_op jit(solution)/shard_map/apply_transposed/pallas_call | solution.py:321
  127.8 12.4 %all_to_all.40.got = f32[16,72,128]{2,1,0:T(8,128)S(1)} all-to-all(f32[16,72,128]{2,1,0:T(8,128)S(1)} %get-tuple-element.57), channel_id=1, replica_groups=mesh['row'=16,'z'=16,'core'=2] {'row'}, dimensions={0} | all-to-all | bytes 1179648 | tf_op jit(solution)/shard_map/all_to_all | solution.py:281
  140.1 0.2 cols.1
  140.3 11.9 %all_to_all.41.vec = f32[16,64,128]{2,1,0:T(8,128)S(1)} all-to-all(f32[16,64,128]{2,1,0:T(8,128)S(1)} %get-tuple-element.61), channel_id=1, replica_groups=mesh['row'=16,'z'=16,'core'=2] {'row'}, dimensions={0} | all-to-all | bytes 1048576 | tf_op jit(solution)/shard_map/all_to_all | solution.py:281
  152.2 2.6 %apply_plain.3 = (f32[16,64,128]{2,1,0:T(8,128)S(1)}, f32[8,128]{1,0:T(8,128)S(1)}) custom-call(s32[3,64]{1,0:T(4,128)S(1)} %get-tuple-element.76.slots.slots0, s32[3,64]{1,0:T(4,128)S(1)} %slice_convert_fusion.slots.slots1, bf16[64,128,128]{2,1,0:T(8,128)(2,1)S(1)} %get-tuple-element.47.hi0, bf16[64,128,128]{2,1,0:T(8,128)(2,1)S(1)} %get-tuple-element.48.lo0, ...), custom_call_target="tpu_custom_call" | custom-call | tf_op jit(solution)/shard_map/apply_plain/pallas_call | solution.py:329
  154.8 25.4 %all_to_all.42.got = f32[16,64,128]{2,1,0:T(8,128)S(1)} all-to-all(f32[16,64,128]{2,1,0:T(8,128)S(1)} %get-tuple-element.64), channel_id=1, replica_groups=mesh['row'=16,'z'=16,'core'=2] {'z'}, dimensions={0} | all-to-all | bytes 1048576 | tf_op jit(solution)/shard_map/all_to_all | solution.py:281
  180.4 29.4 %all_to_all.43 = f32[256,1,128]{2,1,0:T(1,128)S(1)} all-to-all(f32[256,1,128]{2,1,0:T(1,128)S(1)} %broadcast_in_dim.19), channel_id=1, replica_groups=mesh['row'=16,'z'=16,'core'=2] {'row','z'}, dimensions={0} | all-to-all | bytes 262144 | tf_op jit(solution)/shard_map/all_to_all | solution.py:281
  210.1 24.2 %collective-permute-start.2 = (f32[32,128]{1,0:T(8,128)S(1)}, f32[32,128]{1,0:T(8,128)S(1)}, u32[]{:S(2)}, u32[]{:S(2)}) collective-permute-start(f32[32,128]{1,0:T(8,128)S(1)} %slice.33), channel_id=1, source_target_pairs={{0,1},{1,0},{2,3},{3,2},{4,5},{5,4},{6,7},{7,6},{8,9},{9,8},{10,11... | collective-permute-start | bytes 49160 | tf_op jit(solution)/shard_map/ppermute | solution.py:284
  234.3 0.8 collective-permute-done.2
  235.1 0.6 maximum_bitcast_fusion
  (17 shorter events, 0.6 us)
Async XLA Ops:
  1.4 9.6 %collective-permute-start = (f32[40,128]{1,0:T(8,128)S(1)}, f32[40,128]{1,0:T(8,128)S(1)}, u32[]{:S(2)}, u32[]{:S(2)}) collective-permute-start(f32[40,128]{1,0:T(8,128)S(1)} %select_maximum_fusion), channel_id=1, source_target_pairs={{0,1},{1,0},{2,3},{3,2},{4,5},{5,4},{6,7},{7,6},{8,9},{9,8},{10,11... | collective-permute-start | bytes 61448 | tf_op jit(solution)/shard_map/ppermute | solution.py:284
  11.1 28.5 %collective-permute-start.1 = (f32[64,128,128]{2,1,0:T(8,128)}, f32[64,128,128]{2,1,0:T(8,128)S(1)}, u32[]{:S(2)}, u32[]{:S(2)}) collective-permute-start(f32[64,128,128]{2,1,0:T(8,128)} %bitcast.19), channel_id=1, source_target_pairs={{0,1},{1,0},{2,3},{3,2},{4,5},{5,4},{6,7},{7,6},{8,9},{9,8},{10,11... | collective-permute-start | bytes 12582920 | tf_op jit(solution)/shard_map/ppermute | solution.py:284
  39.6 2.3 copy-start
  210.1 25.0 %collective-permute-start.2 = (f32[32,128]{1,0:T(8,128)S(1)}, f32[32,128]{1,0:T(8,128)S(1)}, u32[]{:S(2)}, u32[]{:S(2)}) collective-permute-start(f32[32,128]{1,0:T(8,128)S(1)} %slice.33), channel_id=1, source_target_pairs={{0,1},{1,0},{2,3},{3,2},{4,5},{5,4},{6,7},{7,6},{8,9},{9,8},{10,11... | collective-permute-start | bytes 49160 | tf_op jit(solution)/shard_map/ppermute | solution.py:284
